TPU v7x, 32 devices: a whole 2x2x4 slice. The times are simulated.
32 devices in a mesh: rows: 8 (over z, x), seq: 4 (over y, core).
Axes of the slice: x: 2, y: 2, z: 4, core: 2. Of those that a mesh axis runs over, the one named last changes fastest.
Arguments:
- tokens: bfloat16 [16, 1024, 768], P('rows', 'seq'), may hold values from -6 to 6
- cotangent: bfloat16 [16, 1024, 768], P('rows', 'seq'), may hold values from -6 to 6
- segment_ids: int32 [16, 1024], P('rows'), may hold values from 0 to 1, as said below
- mask_positions: int32 [16, 2, 80], P('rows'), may hold values from -1 to 1023, as said below
- query_weight: bfloat16 [768, 768], replicated, may hold values from -0.21875 to 0.21875
- query_bias: float32 [768], replicated, may hold values from -2 to 2
- key_weight: bfloat16 [768, 768], replicated, may hold values from -0.21875 to 0.21875
- value_weight: bfloat16 [768, 768], replicated, may hold values from -0.21875 to 0.21875
- value_bias: float32 [768], replicated, may hold values from -2 to 2
- output_weight: bfloat16 [768, 768], replicated, may hold values from -3.5 to 3.5
- output_bias: float32 [768], replicated, may hold values from -2 to 2
- first_gain: float32 [768], replicated, may hold values from 0.5 to 1.5
- first_shift: float32 [768], replicated, may hold values from -2 to 2
- up_weight: bfloat16 [768, 3072], replicated, may hold values from -0.21875 to 0.21875
- up_bias: float32 [3072], replicated, may hold values from -2 to 2
- down_weight: bfloat16 [3072, 768], replicated, may hold values from -0.109375 to 0.109375
- down_bias: float32 [768], replicated, may hold values from -2 to 2
- second_gain: float32 [768], replicated, may hold values from 0.5 to 1.5
- second_shift: float32 [768], replicated, may hold values from -2 to 2
Outputs:
- layer_output: bfloat16 [16, 1024, 768], P('rows', 'seq')
- input_grad: float32 [16, 1024, 768], P('rows', 'seq')
- grad_query_weight: float32 [768, 768], replicated
- grad_query_bias: float32 [768], replicated
- grad_key_weight: float32 [768, 768], replicated
- grad_value_weight: float32 [768, 768], replicated
- grad_value_bias: float32 [768], replicated
- grad_output_weight: float32 [768, 768], replicated
- grad_output_bias: float32 [768], replicated
- grad_first_gain: float32 [768], replicated
- grad_first_shift: float32 [768], replicated
- grad_up_weight: float32 [768, 3072], P(None, ('rows', 'seq'))
- grad_up_bias: float32 [3072], replicated
- grad_down_weight: float32 [3072, 768], P(('rows', 'seq'))
- grad_down_bias: float32 [768], replicated
- grad_second_gain: float32 [768], replicated
- grad_second_shift: float32 [768], replicated
Inputs may be any that keep to these rules, and one draw needn't show every extreme that they name: `segment_ids`: each row is 0 up to a split point and 1 after it; both sequences are nonempty and one of them holds more than 768 positions. `mask_positions`: entry [r, s, j] is a masked position of sequence s (0 the first, 1 the second) of row r, counted within the row; each sequence has 1 to 80 distinct masked positions inside it, listed first; remaining entries are -1.
All inputs are finite; a program needn't handle non-finite values.
Results may differ from a plain program's by a relative error of at most 0.013.
The roundings to bfloat16 on the way count: a program that leaves them out, or rounds other values in their place, can miss the bound.
Values may be sent and summed in bfloat16 or wider, within the bound.
A program may use at most 192 MiB of HBM per device.

v0:
```python
import functools

import jax
import jax.numpy as jnp
from jax import lax
from jax.experimental import pallas as pl
from jax.experimental.pallas import tpu as pltpu
from jax.sharding import PartitionSpec as P

HEADS = 12
EPSILON = 1e-12
MASKED_SCORE = -1000000000.0
F32 = jnp.float32
BF16 = jnp.bfloat16
MESH = pl.DeviceIdType.MESH
VMEM_LIMIT = 56 * 2**20


def dot(left, right):
    return lax.dot_general(left, right, (((1,), (0,)), ((), ())), preferred_element_type=F32)


def dot_nt(left, right):
    return lax.dot_general(left, right, (((1,), (1,)), ((), ())), preferred_element_type=F32)


def dot_tn(left, right):
    return lax.dot_general(left, right, (((0,), (0,)), ((), ())), preferred_element_type=F32)


def norm_parts(hidden):
    centred = hidden - jnp.mean(hidden, axis=-1, keepdims=True)
    variance = jnp.mean(centred * centred, axis=-1, keepdims=True)
    scale = lax.rsqrt(variance + EPSILON)
    return centred * scale, scale


def norm_back(grad, normed, scale, gain):
    scaled = grad * gain
    along = jnp.mean(scaled * normed, axis=-1, keepdims=True)
    return (scaled - jnp.mean(scaled, axis=-1, keepdims=True) - normed * along) * scale


GELU_A = 0.7978845608028654
GELU_B = 0.044715


def gelu_parts(value):
    square = value * value
    bent = jnp.tanh(GELU_A * value * (1.0 + GELU_B * square))
    half = 0.5 * (1.0 + bent)
    slope = half + 0.5 * value * (1.0 - bent * bent) * (GELU_A * (1.0 + 3.0 * GELU_B * square))
    return value * half, slope


def gelu_only(value):
    bent = jnp.tanh(GELU_A * value * (1.0 + GELU_B * value * value))
    return 0.5 * value * (1.0 + bent)


def lane_is(shape, low, high):
    lane = lax.broadcasted_iota(jnp.int32, shape, len(shape) - 1)
    return (lane >= low) & (lane < high)


def project_kernel(core, half, peer, pos, seg, slots, wq, bq, wk, wv, bv, keys, values, queries, context, probs, picked):
    width = keys.shape[1]
    mine = pl.ds(pl.multiple_of(core[0] * width, 128), width)
    count = slots.shape[0]
    tokens_half = half.shape[0]
    chosen = jnp.where(slots[...] == pos[...], 1.0, 0.0).astype(BF16)
    rows = dot(chosen[:, :tokens_half], half[...]) + dot(chosen[:, tokens_half:], peer[...])
    rows = rows.astype(BF16)
    picked[...] = rows
    queries[...] = (dot(rows, wq[:, mine]) + bq[:, mine]).astype(BF16)
    for place, part in ((0, half), (tokens_half, peer)):
        for start in range(0, tokens_half, 256):
            block = part[start : start + 256, :]
            there = slice(place + start, place + start + 256)
            keys[there, :] = dot(block, wk[:, mine]).astype(BF16)
            values[there, :] = (dot(block, wv[:, mine]) + bv[:, mine]).astype(BF16)
    sequence = lax.broadcasted_iota(jnp.int32, (count, 1), 0) // (count // 2)
    same = seg[...] == sequence
    for pair in range(width // 128):
        lanes = slice(pair * 128, pair * 128 + 128)
        pair_queries = queries[:, lanes].astype(F32) * 0.125
        pair_keys, pair_values = keys[:, lanes], values[:, lanes]
        outs = []
        for side in range(2):
            keep = lane_is((count, 128), side * 64, side * 64 + 64)
            head_queries = jnp.where(keep, pair_queries, 0.0).astype(BF16)
            scores = jnp.where(same, dot_nt(head_queries, pair_keys), MASKED_SCORE)
            weights = jnp.exp(scores - jnp.max(scores, axis=-1, keepdims=True))
            share = weights / jnp.sum(weights, axis=-1, keepdims=True)
            probs[pair * 2 + side] = share
            outs.append(dot(share.astype(BF16), pair_values))
        first = lane_is((count, 128), 0, 64)
        context[:, lanes] = jnp.where(first, outs[0], outs[1]).astype(BF16)


def masked_kernel(core, ctx_own, ctx_peer, picked, cot_half, cot_peer, pos, slots, wo, bo, g1, s1, wup, bup, wdown, bdown, g2, s2, normed_low, feed, branch_low, grad_h1, small):
    count, width = ctx_own.shape
    hidden = wup.shape[1]
    model = wup.shape[0]
    tokens_half = cot_half.shape[0]
    mine = pl.multiple_of(core[0] * count, 16)
    is_first = core[0] == 0
    left = jnp.where(is_first, ctx_own[...], ctx_peer[...])
    right = jnp.where(is_first, ctx_peer[...], ctx_own[...])
    branch = dot(left, wo[:width, :]) + dot(right, wo[width:, :]) + bo[...]
    h1 = picked[pl.ds(mine, count), :].astype(F32) + branch
    n1, r1 = norm_parts(h1)
    y1 = n1 * g1[...] + s1[...]
    y1_low = y1.astype(BF16)
    normed_low[...] = y1_low
    total = y1 + bdown[...]
    slopes = []
    step = model
    for start in range(0, hidden, step):
        pre = dot(y1_low, wup[:, start : start + step]) + bup[:, start : start + step]
        act, slope = gelu_parts(pre)
        slopes.append(slope)
        total = total + dot(act.astype(BF16), wdown[start : start + step, :])
    n2, r2 = norm_parts(total)
    chosen = jnp.where(slots[pl.ds(mine, count), :] == pos[...], 1.0, 0.0).astype(BF16)
    grad = dot(chosen[:, :tokens_half], cot_half[...]) + dot(chosen[:, tokens_half:], cot_peer[...])
    gh2 = norm_back(grad, n2, r2, g2[...])
    gf = gh2.astype(BF16)
    feed[...] = gf
    gy1 = gh2
    small[...] = jnp.zeros_like(small)
    for place, start in enumerate(range(0, hidden, step)):
        ga = dot_nt(gf, wdown[start : start + step, :])
        gp = (ga * slopes[place]).astype(BF16)
        small[place : place + 1, :] = jnp.sum(gp.astype(F32), axis=0, keepdims=True)
        gy1 = gy1 + dot_nt(gp, wup[:, start : start + step])
    gh1 = norm_back(gy1, n1, r1, g1[...])
    grad_h1[...] = gh1
    gb = gh1.astype(BF16)
    branch_low[...] = gb
    base = hidden // step
    for place, value in enumerate((gy1 * n1, gy1, grad * n2, grad, gb.astype(F32), gf.astype(F32))):
        small[base + place : base + place + 1, :] = jnp.sum(value, axis=0, keepdims=True)


def back_kernel(core, keys, values, queries, context, probs, picked, gb_own, gb_peer, gh1, half, peer, pos_col, slots_row, wq, wk, wv, wo, grads, igrad_own, igrad_peer, bias, dq_low, dk_low, dv_low):
    width = keys.shape[1]
    count = queries.shape[0]
    own = gb_own.shape[0]
    tokens_half = half.shape[0]
    is_first = core[0] == 0
    mine = pl.ds(pl.multiple_of(core[0] * width, 128), width)
    mine_rows = pl.ds(pl.multiple_of(core[0] * width, 128), width)
    top = jnp.where(is_first, gb_own[...], gb_peer[...])
    low = jnp.where(is_first, gb_peer[...], gb_own[...])
    gb = jnp.concatenate([top, low], axis=0)
    gctx = dot_nt(gb, wo[mine_rows, :]).astype(BF16)
    for pair in range(width // 128):
        lanes = slice(pair * 128, pair * 128 + 128)
        pair_keys, pair_values, pair_queries = keys[:, lanes], values[:, lanes], queries[:, lanes]
        pair_gctx = gctx[:, lanes]
        dqs, dks, dvs = [], [], []
        for side in range(2):
            keep = lane_is((count, 128), side * 64, side * 64 + 64)
            head_gctx = jnp.where(keep, pair_gctx.astype(F32), 0.0).astype(BF16)
            share = probs[pair * 2 + side]
            gp = dot_nt(head_gctx, pair_values)
            spread = jnp.sum(share * gp, axis=-1, keepdims=True)
            gs = (share * (gp - spread)).astype(BF16)
            dqs.append(dot(gs, pair_keys))
            dks.append(dot_tn(gs, pair_queries))
            dvs.append(dot_tn(share.astype(BF16), pair_gctx))
        first = lane_is((count, 128), 0, 64)
        dq_low[:, lanes] = (jnp.where(first, dqs[0], dqs[1]) * 0.125).astype(BF16)
        first = lane_is((2 * tokens_half, 128), 0, 64)
        dk_low[:, lanes] = (jnp.where(first, dks[0], dks[1]) * 0.125).astype(BF16)
        dv_low[:, lanes] = jnp.where(first, dvs[0], dvs[1]).astype(BF16)
    grads[1] = dot_tn(picked[...], dq_low[...]).astype(BF16)
    gwo = dot_tn(context[...], gb).astype(BF16)
    grads[0, :width, :] = gwo[:, :width]
    grads[0, width:, :] = gwo[:, width:]
    for place, part in ((2, dk_low), (3, dv_low)):
        total = dot_tn(half[...], part[:tokens_half, :]) + dot_tn(peer[...], part[tokens_half:, :])
        grads[place] = total.astype(BF16)
    bias[0:1, :] = jnp.sum(dq_low[...].astype(F32), axis=0, keepdims=True)
    bias[1:2, :] = jnp.sum(dv_low[...].astype(F32), axis=0, keepdims=True)
    spread_rows = dot_nt(dq_low[...], wq[:, mine])
    zero = jnp.zeros((own, wq.shape[0]), F32)
    spread_rows = spread_rows + jnp.concatenate(
        [jnp.where(is_first, gh1[...], zero), jnp.where(is_first, zero, gh1[...])], axis=0
    )
    high = spread_rows.astype(BF16)
    rest = (spread_rows - high.astype(F32)).astype(BF16)
    for start in range(0, 2 * tokens_half, 256):
        here = slice(start, start + 256)
        chosen = jnp.where(pos_col[here, :] == slots_row[...], 1.0, 0.0).astype(BF16)
        total = dot(chosen, high) + dot(chosen, rest)
        total = total + dot_nt(dk_low[here, :], wk[:, mine]) + dot_nt(dv_low[here, :], wv[:, mine])
        if start < tokens_half:
            igrad_own[here, :] = total
        else:
            igrad_peer[start - tokens_half : start - tokens_half + 256, :] = total.astype(BF16)


def attend_kernel(core, half, peer, seg, seg_col, keys, values, wq, bq, own, other):
    width = keys.shape[1]
    mine = pl.ds(pl.multiple_of(core[0] * width, 128), width)
    tile = 256
    for part, out in ((half, own), (peer, other)):
        place = 0 if part is half else half.shape[0]

        def body(step, carry, part=part, out=out, place=place):
            here = pl.ds(pl.multiple_of(step * tile, tile), tile)
            queries = (dot(part[here, :], wq[:, mine]) + bq[:, mine]).astype(BF16).astype(F32) * 0.125
            same = seg_col[pl.ds(pl.multiple_of(place + step * tile, tile), tile), :] == seg[...]
            for pair in range(width // 128):
                lanes = slice(pair * 128, pair * 128 + 128)
                outs = []
                for side in range(2):
                    keep = lane_is((tile, 128), side * 64, side * 64 + 64)
                    head_queries = jnp.where(keep, queries[:, lanes], 0.0).astype(BF16)
                    scores = jnp.where(same, dot_nt(head_queries, keys[:, lanes]), MASKED_SCORE)
                    weights = jnp.exp(scores - jnp.max(scores, axis=-1, keepdims=True))
                    total = jnp.sum(weights, axis=-1, keepdims=True)
                    outs.append(dot(weights.astype(BF16), values[:, lanes]) / total)
                first = lane_is((tile, 128), 0, 64)
                out[here, lanes] = jnp.where(first, outs[0], outs[1]).astype(BF16)
            return carry

        lax.fori_loop(0, part.shape[0] // tile, body, 0)


def feed_kernel(core, ctx_own, ctx_peer, half, wo, bo, g1, s1, wup, bup, wdown, bdown, g2, s2, own, other):
    width = ctx_own.shape[1]
    hidden, model = wdown.shape
    is_first = core[0] == 0
    tile = own.shape[0]
    for start, out in ((0, own), (tile, other)):
        here = slice(start, start + tile)
        left = jnp.where(is_first, ctx_own[here, :], ctx_peer[here, :])
        right = jnp.where(is_first, ctx_peer[here, :], ctx_own[here, :])
        branch = dot(left, wo[:width, :]) + dot(right, wo[width:, :]) + bo[...]
        n1, _ = norm_parts(half[here, :].astype(F32) + branch)
        y1 = n1 * g1[...] + s1[...]
        y1_low = y1.astype(BF16)
        total = y1 + bdown[...]
        for place in range(0, hidden, model):
            pre = dot(y1_low, wup[:, place : place + model]) + bup[:, place : place + model]
            total = total + dot(gelu_only(pre).astype(BF16), wdown[place : place + model, :])
        n2, _ = norm_parts(total)
        out[...] = (n2 * g2[...] + s2[...]).astype(BF16)


def hidden_kernel(slot, normed, feed, wup, bup, wdown, out):
    units = out.shape[0]
    model = normed.shape[1]
    mine = pl.ds(pl.multiple_of(slot[0] * units, 128), units)
    pre = dot(normed[...], wup[:, mine]) + bup[:, mine]
    act, slope = gelu_parts(pre)
    ga = dot_nt(feed[...], wdown[mine, :])
    gp = (ga * slope).astype(BF16)
    out[:, :model] = dot_tn(gp, normed[...]).astype(BF16)
    out[:, model:] = dot_tn(act.astype(BF16), feed[...]).astype(BF16)


def place_here():
    row, seq = lax.axis_index("rows"), lax.axis_index("seq")
    return row // 2, row % 2, seq // 2, seq % 2


def device(z, x, y, core):
    return (z * 2 + x, y * 2 + core)


def layer_kernel(
    tokens, cotangent, segments, slots, vecs, wq, wk, wv, wo, wup, wdown,
    layer_out, input_grad, out_o, out_q, out_k, out_v, hidden_out, small_out,
    xs, cs, wq_v, wk_v, wv_v, wo_v, wup_v, wdown_v, keys, values, queries, context, probs, picked, chosen, ctx_both, gb_both,
    slopes, dq_low, dkv_low, grads, hidden_grads, hidden_in, fac_normed, fac_feed, grad_h1, small_in, small_z,
    all_queries, all_context, ctx_in, total, y1_keep, out_send, dx_send, dx_in, dx_own, igrad_send, igrad_in,
    in_o, in_q, in_k, in_v, mid_o, mid_q, mid_k, mid_v, local_sem, send_sem, recv_sem,
):
    z, x, y, core = place_here()
    row = y
    stretch, model = tokens.shape[1:]
    half = 2 * stretch
    full = 2 * half
    width = wq_v.shape[1]
    masks = slots.shape[2]
    count = 2 * masks
    hidden = wup.shape[1]
    parts = hidden // model
    units = hidden_out.shape[0]
    others = [(z + k) % 4 for k in (1, 2, 3)]
    at_y, at_x, twin = device(z, x, 1 - y, core), device(z, 1 - x, y, core), device(z, x, y, 1 - core)
    columns = [device(o, x, y, core) for o in others]
    mine = pl.ds(pl.multiple_of(core * width, 128), width)
    my_slots = pl.ds(pl.multiple_of(core * masks, 16), masks)
    twin_slots = pl.ds(pl.multiple_of((1 - core) * masks, 16), masks)
    pending = []

    def local(src, dst, index):
        copy = pltpu.make_async_copy(src, dst, local_sem.at[index])
        copy.start()
        return copy

    def remote(src, dst, index, target):
        return pltpu.make_async_remote_copy(
            src_ref=src, dst_ref=dst, send_sem=send_sem.at[index], recv_sem=recv_sem.at[index],
            device_id=target, device_id_type=MESH,
        )

    def push(src, dst, index, target):
        copy = remote(src, dst, index, target)
        copy.start()
        pending.append(copy)
        return copy

    def vector(index):
        return vecs[index : index + 1, :]

    def half_vector(index):
        return vecs[index : index + 1, mine]

    own_tokens = local(tokens.at[row], xs.at[pl.ds(0, stretch)], 0)
    get_wk = local(wk.at[:, mine], wk_v, 1)
    get_wv = local(wv.at[:, mine], wv_v, 2)
    get_wq = local(wq.at[:, mine], wq_v, 3)
    own_cot = local(cotangent.at[row], cs.at[pl.ds(0, stretch)], 4)
    get_wo = local(wo, wo_v, 5)
    get_up = local(wup, wup_v, 6)
    get_down = local(wdown, wdown_v, 7)

    barrier = pltpu.get_barrier_semaphore()
    for cx in range(2):
        for cy in range(2):
            for cc in range(2):
                @pl.when(jnp.logical_not((cx == x) & (cy == y) & (cc == core)))
                def _(cx=cx, cy=cy, cc=cc):
                    pl.semaphore_signal(barrier, inc=1, device_id=device(z, cx, cy, cc), device_id_type=MESH)
    for target in columns:
        pl.semaphore_signal(barrier, inc=1, device_id=target, device_id_type=MESH)
    pl.semaphore_wait(barrier, 10)

    piece = stretch // 2
    tok_y = [
        push(tokens.at[1 - row, pl.ds(k * piece, piece)], xs.at[pl.ds(stretch + k * piece, piece)], k, at_y) for k in range(2)
    ]
    tok_c = push(tokens.at[row], xs.at[pl.ds(half, stretch)], 2, twin)
    cot_y = push(cotangent.at[1 - row], cs.at[pl.ds(stretch, stretch)], 3, at_y)
    cot_c = push(cotangent.at[row], cs.at[pl.ds(half, stretch)], 4, twin)

    def key_values(start):
        here = pl.ds(start, stretch)
        block = xs[here, :]
        keys[here, :] = dot(block, wk_v[...]).astype(BF16)
        values[here, :] = (dot(block, wv_v[...]) + half_vector(5)).astype(BF16)

    blocks = [2 * y + core, 2 * (1 - y) + core, 2 * y + 1 - core, 2 * (1 - y) + 1 - core]
    lane = lax.broadcasted_iota(jnp.int32, (1, stretch), 1)
    pos_row = jnp.concatenate([lane + block * stretch for block in blocks], axis=1)
    seg_here = segments[pl.ds(row, 1), :]
    split = jnp.sum((1 - seg_here).astype(F32), axis=1, keepdims=True)
    pos_row = pos_row.astype(F32)
    seg_row = jnp.where(pos_row >= split, 1.0, 0.0)
    slot_rows = slots[row].astype(F32)
    diagonal = lax.broadcasted_iota(jnp.int32, (masks, masks), 0) == lax.broadcasted_iota(jnp.int32, (masks, masks), 1)
    for sequence in range(2):
        column = jnp.sum(jnp.where(diagonal, slot_rows[sequence : sequence + 1, :], 0.0), axis=1, keepdims=True)
        chosen[sequence * masks : (sequence + 1) * masks, :] = jnp.where(column == pos_row, 1.0, 0.0).astype(BF16)

    own_tokens.wait()
    get_wk.wait()
    get_wv.wait()
    key_values(0)
    tok_c.wait_recv()
    key_values(half)
    forward = []
    for k in range(2):
        tok_y[k].wait_recv()
        src = xs.at[pl.ds(stretch + k * piece, piece)]
        forward.append(push(src, xs.at[pl.ds(half + stretch + k * piece, piece)], 5 + k, twin))
    key_values(stretch)
    for copy in forward:
        copy.wait_recv()
    key_values(half + stretch)

    rows = dot(chosen[...], xs[...]).astype(BF16)
    picked[...] = rows
    get_wq.wait()
    queries[...] = (dot(rows, wq_v[...]) + half_vector(4)).astype(BF16)
    sequence = lax.broadcasted_iota(jnp.int32, (count, 1), 0) // masks
    same = seg_row == sequence.astype(F32)
    pairs = width // 128
    for pair in range(pairs):
        lanes = slice(pair * 128, pair * 128 + 128)
        pair_queries = queries[:, lanes].astype(F32) * 0.125
        pair_keys, pair_values = keys[:, lanes], values[:, lanes]
        outs = []
        for side in range(2):
            keep = lane_is((count, 128), side * 64, side * 64 + 64)
            head_queries = jnp.where(keep, pair_queries, 0.0).astype(BF16)
            scores = jnp.where(same, dot_nt(head_queries, pair_keys), MASKED_SCORE)
            weights = jnp.exp(scores - jnp.max(scores, axis=-1, keepdims=True))
            share = weights / jnp.sum(weights, axis=-1, keepdims=True)
            probs[pair * 2 + side] = share
            outs.append(dot(share.astype(BF16), pair_values))
        first = lane_is((count, 128), 0, 64)
        context[:, lanes] = jnp.where(first, outs[0], outs[1]).astype(BF16)
    ctx_both[core] = context[my_slots, :]
    ctx_c = push(context.at[twin_slots], ctx_both.at[core], 7, twin)

    own_cot.wait()
    cot_y.wait_recv()
    cot_f = push(cs.at[pl.ds(stretch, stretch)], cs.at[pl.ds(half + stretch, stretch)], 8, twin)
    for start in range(0, full, stretch):
        value = (dot(xs[start : start + stretch, :], wq_v[...]) + half_vector(4)).astype(BF16)
        all_queries[start : start + stretch, :] = (value.astype(F32) * 0.125).astype(BF16)
    get_wo.wait()
    ctx_c.wait_recv()

    branch = dot(ctx_both[0], wo_v[:width, :]) + dot(ctx_both[1], wo_v[width:, :]) + vector(6)
    n1, r1 = norm_parts(picked[my_slots, :].astype(F32) + branch)
    y1 = n1 * vector(7) + vector(8)
    y1_low = y1.astype(BF16)
    fac_normed[core, z] = y1_low
    spot = fac_normed.at[core, z]
    norm_z = [push(spot, spot, 9 + k, columns[k]) for k in range(3)]
    get_up.wait()
    get_down.wait()
    sum2 = y1 + vector(9)
    for part in range(parts):
        there = slice(part * model, (part + 1) * model)
        act, slope = gelu_parts(dot(y1_low, wup_v[:, there]) + vector(part))
        slopes[part] = slope
        sum2 = sum2 + dot(act.astype(BF16), wdown_v[there, :])
    n2, r2 = norm_parts(sum2)
    cot_c.wait_recv()
    cot_f.wait_recv()
    grad = dot(chosen[my_slots, :], cs[...])
    gh2 = norm_back(grad, n2, r2, vector(10))
    gf = gh2.astype(BF16)
    fac_feed[core, z] = gf
    spot = fac_feed.at[core, z]
    feed_z = [push(spot, spot, 12 + k, columns[k]) for k in range(3)]
    gy1 = gh2
    small_in[0] = jnp.zeros(small_in.shape[1:], F32)
    for part in range(parts):
        there = slice(part * model, (part + 1) * model)
        gp = (dot_nt(gf, wdown_v[there, :]) * slopes[part]).astype(BF16)
        small_in[0, part : part + 1, :] = jnp.sum(gp.astype(F32), axis=0, keepdims=True)
        gy1 = gy1 + dot_nt(gp, wup_v[:, there])
    gh1 = norm_back(gy1, n1, r1, vector(7))
    grad_h1[...] = gh1
    gb = gh1.astype(BF16)
    gb_both[core] = gb
    gb_c = push(gb_both.at[core], gb_both.at[core], 15, twin)
    for place, value in enumerate((gy1 * n1, gy1, grad * n2, grad, gb.astype(F32), gf.astype(F32))):
        small_in[0, parts + place : parts + place + 1, :] = jnp.sum(value, axis=0, keepdims=True)
    gb_c.wait_recv()

    spots = {"x": x, "y": y, "z": z}
    sizes = {"x": 2, "y": 2, "z": 4}
    dims = {"x": [at_x], "y": [at_y], "z": columns}
    orders = ["xyz", "zyx", "xyz", "xyz"]
    ins = [in_o, in_q, in_k, in_v]
    mids = [mid_o, mid_q, mid_k, mid_v]
    outs = [out_o, out_q, out_k, out_v]

    def regions(job):
        base, size, found = 0, model, [(0, model)]
        for dim in orders[job]:
            size = size // sizes[dim]
            base = base + spots[dim] * size
            found.append((base, size))
        return found

    def in_place(job, stage):
        at, size = 0, model
        for dim in orders[job][:stage]:
            size = size // sizes[dim]
            at += size * (sizes[dim] - 1)
        return at, size // sizes[orders[job][stage]]

    def mid_place(job, stage):
        at, size = 0, model
        for dim in orders[job][:stage]:
            size = size // sizes[dim]
            at += size
        return at

    def out_at(job, base, size):
        if job == 0:
            side = base // width
            offset = base - side * width
            at = pl.ds(pl.multiple_of(core * width + offset, 16), size)
            return outs[0].at[at, pl.ds(pl.multiple_of(side * width, 128), width)]
        return outs[job].at[pl.ds(pl.multiple_of(base, 16), size), mine]

    def reduce_copies(job, stage):
        dim = orders[job][stage]
        at, size = in_place(job, stage)
        copies = []
        for k, target in enumerate(dims[dim]):
            other = (spots[dim] + k + 1) % sizes[dim]
            if stage == 0:
                src = grads.at[job, pl.ds(pl.multiple_of(other * size, 16), size)]
            else:
                src = mids[job].at[pl.ds(pl.multiple_of(mid_place(job, stage - 1) + other * size, 16), size)]
            dst = ins[job].at[pl.ds(at + k * size, size)]
            copies.append(remote(src, dst, 40 + job * 20 + stage * 3 + k, target))
        return copies

    def reduce_start(job, stage):
        for copy in reduce_copies(job, stage):
            copy.start()

    def reduce_end(job, stage):
        for copy in reduce_copies(job, stage):
            copy.wait()
        dim = orders[job][stage]
        at, size = in_place(job, stage)
        here = spots[dim] * size
        if stage == 0:
            value = grads[job, pl.ds(pl.multiple_of(here, 16), size)].astype(F32)
        else:
            value = mids[job][pl.ds(pl.multiple_of(mid_place(job, stage - 1) + here, 16), size)].astype(F32)
        for k in range(len(dims[dim])):
            value = value + ins[job][pl.ds(at + k * size, size)].astype(F32)
        value = value.astype(BF16)
        if stage < 2:
            mids[job][pl.ds(mid_place(job, stage), size)] = value
            reduce_start(job, stage + 1)
        else:
            base, _ = regions(job)[3]
            out_at(job, base, size)[...] = value
            gather_start(job, 2)

    def gather_copies(job, stage):
        base, size = regions(job)[stage + 1]
        spot = out_at(job, base, size)
        return [
            remote(spot, spot, 40 + job * 20 + 9 + stage * 3 + k, target)
            for k, target in enumerate(dims[orders[job][stage]])
        ]

    def twin_copy(job):
        spot = outs[0].at[mine, :] if job == 0 else outs[job].at[:, mine]
        return remote(spot, spot, 40 + job * 20 + 18, twin)

    def gather_start(job, stage):
        for copy in gather_copies(job, stage):
            copy.start()

    def gather_end(job, stage):
        for copy in gather_copies(job, stage):
            copy.wait()
        if stage > 0:
            gather_start(job, stage - 1)
        else:
            twin_copy(job).start()

    def small_copies(stage):
        if stage < 3:
            target = (twin, at_y, at_x)[stage]
            return [remote(small_in.at[2 * stage], small_in.at[2 * stage + 1], 16 + stage, target)]
        return [remote(small_in.at[6], small_z.at[z], 19 + k, target) for k, target in enumerate(columns)]

    def small_start(stage):
        for copy in small_copies(stage):
            copy.start()

    def small_end(stage):
        for copy in small_copies(stage):
            copy.wait()
        if stage < 3:
            small_in[2 * stage + 2] = small_in[2 * stage] + small_in[2 * stage + 1]
            if stage == 2:
                small_z[z] = small_in[6]
            small_start(stage + 1)
        else:
            small_out[...] = (small_z[0] + small_z[1]) + (small_z[2] + small_z[3])

    source = x * 2 + y

    def factor_copies():
        return [remote(ref.at[core], ref.at[core], 22 + k, twin) for k, ref in enumerate((fac_normed, fac_feed))]

    def factors_on():
        for copy in norm_z + feed_z:
            copy.wait_recv()
        for copy in factor_copies():
            copy.start()

    def is_me(cy, cc):
        return (core == x) & (cy == y) & (cc == core)

    def hidden_copy(cy, cc):
        part = hidden_grads.at[pl.ds((cy * 2 + cc) * units, units)]
        return pltpu.make_async_remote_copy(
            src_ref=part, dst_ref=hidden_in.at[source], send_sem=send_sem.at[24 + cy * 2 + cc], recv_sem=recv_sem.at[24 + source],
            device_id=device(z, core, cy, cc), device_id_type=MESH,
        )

    def hidden_make():
        for copy in factor_copies():
            copy.wait()
        slot = z * 2 + core
        size = hidden_grads.shape[0]
        normed = fac_normed[...].reshape(8 * masks, model)
        feed = fac_feed[...].reshape(8 * masks, model)
        at = pl.ds(pl.multiple_of(slot * size, 128), size)
        act, slope = gelu_parts(dot(normed, wup_v[:, at]) + vecs[pl.ds(z, 1), mine])
        gp = (dot_nt(feed, wdown_v[at, :]) * slope).astype(BF16)
        hidden_grads[:, :model] = dot_tn(gp, normed).astype(BF16)
        hidden_grads[:, model:] = dot_tn(act.astype(BF16), feed).astype(BF16)
        for cy in range(2):
            for cc in range(2):
                @pl.when(jnp.logical_not(is_me(cy, cc)))
                def _(cy=cy, cc=cc):
                    hidden_copy(cy, cc).start()

                @pl.when(is_me(cy, cc))
                def _(cy=cy, cc=cc):
                    hidden_in[source] = hidden_grads[pl.ds((cy * 2 + cc) * units, units)]

    def hidden_end():
        for cy in range(2):
            for cc in range(2):
                @pl.when(jnp.logical_not(is_me(cy, cc)))
                def _(cy=cy, cc=cc):
                    hidden_copy(cy, cc).wait_send()
        for cx in range(2):
            for cy in range(2):
                @pl.when(jnp.logical_not((cx == x) & (cy == y) & (core == x)))
                def _(cx=cx, cy=cy):
                    slot = hidden_in.at[cx * 2 + cy]
                    pltpu.make_async_remote_copy(
                        src_ref=slot, dst_ref=slot, send_sem=send_sem.at[24], recv_sem=recv_sem.at[24 + cx * 2 + cy],
                        device_id=twin, device_id_type=MESH,
                    ).wait_recv()
        value = hidden_in[0].astype(F32)
        for k in range(1, 4):
            value = value + hidden_in[k].astype(F32)
        hidden_out[...] = value

    gb = gb_both[...].reshape(count, model)
    gctx = dot_nt(gb, wo_v[mine, :]).astype(BF16)
    value = dot_tn(context[...], gb).astype(BF16)
    grads[0, :width, :] = value[:, :width]
    grads[0, width:, :] = value[:, width:]
    reduce_start(0, 0)
    for pair in range(pairs):
        lanes = slice(pair * 128, pair * 128 + 128)
        pair_keys, pair_values, pair_queries = keys[:, lanes], values[:, lanes], queries[:, lanes]
        pair_gctx = gctx[:, lanes]
        dqs, dks, dvs = [], [], []
        for side in range(2):
            keep = lane_is((count, 128), side * 64, side * 64 + 64)
            head_gctx = jnp.where(keep, pair_gctx.astype(F32), 0.0).astype(BF16)
            share = probs[pair * 2 + side]
            gp = dot_nt(head_gctx, pair_values)
            spread = jnp.sum(share * gp, axis=-1, keepdims=True)
            gs = (share * (gp - spread)).astype(BF16)
            dqs.append(dot(gs, pair_keys))
            dks.append(dot_tn(gs, pair_queries))
            dvs.append(dot_tn(share.astype(BF16), pair_gctx))
        first = lane_is((count, 128), 0, 64)
        dq_low[:, lanes] = (jnp.where(first, dqs[0], dqs[1]) * 0.125).astype(BF16)
        first = lane_is((full, 128), 0, 64)
        dkv_low[:, lanes] = (jnp.where(first, dks[0], dks[1]) * 0.125).astype(BF16)
        dkv_low[:, width + pair * 128 : width + pair * 128 + 128] = jnp.where(first, dvs[0], dvs[1]).astype(BF16)
        if pair == 0:
            factors_on()
        if pair == 1:
            reduce_end(0, 0)
    for start in range(0, model, 256):
        value = dot_tn(xs[:, start : start + 256], dkv_low[...]).astype(BF16)
        grads[2, start : start + 256, :] = value[:, :width]
        grads[3, start : start + 256, :] = value[:, width:]
    reduce_start(2, 0)
    reduce_start(3, 0)
    grads[1] = dot_tn(picked[...], dq_low[...]).astype(BF16)
    reduce_start(1, 0)
    reduce_end(0, 1)
    small_in[0, parts + 6 : parts + 7, mine] = jnp.sum(dq_low[...].astype(F32), axis=0, keepdims=True)
    small_in[0, parts + 7 : parts + 8, mine] = jnp.sum(dkv_low[:, width:].astype(F32), axis=0, keepdims=True)
    small_start(0)

    spread_rows = dot_nt(dq_low[...], wq_v[...])
    zero = jnp.zeros((masks, model), F32)
    is_first = core == 0
    gh1 = grad_h1[...]
    spread_rows = spread_rows + jnp.concatenate([jnp.where(is_first, gh1, zero), jnp.where(is_first, zero, gh1)], axis=0)
    high = spread_rows.astype(BF16)
    rest = (spread_rows - high.astype(F32)).astype(BF16)
    dx_c = None
    for start in (half, half + stretch, 0, stretch):
        here = slice(start, start + stretch)
        value = dot_tn(chosen[:, here], high) + dot_tn(chosen[:, here], rest)
        value = value + dot_nt(dkv_low[here, :width], wk_v[...]) + dot_nt(dkv_low[here, width:], wv_v[...])
        if start < half:
            dx_own[here, :] = value
        else:
            dx_send[start - half : start - half + stretch, :] = value.astype(BF16)
            if start > half:
                dx_c = push(dx_send, dx_in, 28, twin)

    igrad_copy = remote(igrad_send, igrad_in, 29, at_y)

    def igrad_step():
        dx_c.wait_recv()
        input_grad[row] = dx_own[:stretch, :] + dx_in[:stretch, :].astype(F32)
        igrad_send[...] = (dx_own[stretch:, :] + dx_in[stretch:, :].astype(F32)).astype(BF16)
        remote(igrad_send, igrad_in, 29, at_y).start()

    hidden_make()

    def hooks(step, table):
        for at, actions in table.items():
            @pl.when(step == at)
            def _(actions=actions):
                for action in actions:
                    action[0](*action[1:])

    def ctx_copy():
        return remote(all_context.at[pl.ds(half, half)], ctx_in, 30, twin)

    attend_table = {
        0: [(reduce_end, 2, 0), (small_end, 0)],
        1: [(reduce_end, 1, 0), (igrad_step,)],
        2: [(reduce_end, 0, 2), (small_end, 1)],
        3: [(reduce_end, 3, 0), (reduce_end, 2, 1)],
        4: [(gather_end, 0, 2), (reduce_end, 1, 1)],
        5: [(reduce_end, 2, 2), (small_end, 2)],
        6: [(reduce_end, 3, 1), (gather_end, 0, 1)],
        7: [(reduce_end, 1, 2), (gather_end, 2, 2)],
        8: [(reduce_end, 3, 2), (small_end, 3)],
        9: [(gather_end, 2, 1), (gather_end, 1, 2)],
        10: [(gather_end, 3, 2)],
        11: [(gather_end, 0, 0), (gather_end, 1, 1)],
    }
    feed_table = {
        1: [(gather_end, 3, 1)],
        3: [(gather_end, 2, 0)],
        5: [(gather_end, 1, 0)],
        6: [(hidden_end,)],
    }

    def attend_step(step, carry):
        tile, pair = (step // pairs + 2) % 4, step % pairs
        here = pl.ds(pl.multiple_of(tile * stretch, stretch), stretch)
        lanes = pl.ds(pl.multiple_of(pair * 128, 128), 128)
        block = 2 * (y + (tile % 2) * (1 - 2 * y)) + core + (tile // 2) * (1 - 2 * core)
        place = lax.broadcasted_iota(jnp.int32, (stretch, 1), 0) + block * stretch
        seg_col = jnp.where(place.astype(F32) >= split, 1.0, 0.0)
        same_here = seg_col == seg_row
        pair_queries = all_queries[here, lanes].astype(F32)
        pair_keys, pair_values = keys[:, lanes], values[:, lanes]
        found = []
        for side in range(2):
            keep = lane_is((stretch, 128), side * 64, side * 64 + 64)
            head_queries = jnp.where(keep, pair_queries, 0.0).astype(BF16)
            scores = jnp.where(same_here, dot_nt(head_queries, pair_keys), MASKED_SCORE)
            weights = jnp.exp(scores - jnp.max(scores, axis=-1, keepdims=True))
            found.append(dot(weights.astype(BF16), pair_values) / jnp.sum(weights, axis=-1, keepdims=True))
        first = lane_is((stretch, 128), 0, 64)
        all_context[here, lanes] = jnp.where(first, found[0], found[1]).astype(BF16)

        @pl.when(step == 2 * pairs - 1)
        def _():
            ctx_copy().start()

        hooks(step, attend_table)
        return carry

    lax.fori_loop(0, 4 * pairs, attend_step, 0)
    ctx_copy().wait()

    def out_copy():
        return remote(out_send, layer_out.at[row], 31, at_y)

    def feed_step(step, carry):
        tile, part = 1 - step // parts, step % parts
        here = pl.ds(pl.multiple_of(tile * stretch, stretch), stretch)

        @pl.when(part == 0)
        def _():
            left = jnp.where(is_first, all_context[here, :], ctx_in[here, :])
            right = jnp.where(is_first, ctx_in[here, :], all_context[here, :])
            here_branch = dot(left, wo_v[:width, :]) + dot(right, wo_v[width:, :]) + vector(6)
            normed, _ = norm_parts(xs[here, :].astype(F32) + here_branch)
            value = normed * vector(7) + vector(8)
            y1_keep[...] = value.astype(BF16)
            total[...] = value + vector(9)

        there = pl.ds(pl.multiple_of(part * model, model), model)
        pre = dot(y1_keep[...], wup_v[:, there]) + vecs[pl.ds(part, 1), :]
        total[...] += dot(gelu_only(pre).astype(BF16), wdown_v[there, :])

        @pl.when(part == parts - 1)
        def _():
            normed, _ = norm_parts(total[...])
            value = (normed * vector(10) + vector(11)).astype(BF16)

            @pl.when(tile == 1)
            def _():
                out_send[...] = value
                out_copy().start()

            @pl.when(tile == 0)
            def _():
                layer_out[row] = value

        hooks(step, feed_table)
        return carry

    lax.fori_loop(0, 2 * parts, feed_step, 0)
    gather_end(3, 0)
    igrad_copy.wait()
    input_grad[1 - row] = igrad_in[...].astype(F32)
    out_copy().wait()
    for job in range(4):
        twin_copy(job).wait()
    for copy in pending:
        copy.wait_send()


def vmem(count):
    return [pl.BlockSpec(memory_space=pltpu.VMEM)] * count


def local_call(body, outs, name, scratch=()):
    def call(core, *operands):
        return pl.pallas_call(
            body,
            out_shape=outs,
            in_specs=[pl.BlockSpec(memory_space=pltpu.SMEM)] + vmem(len(operands)),
            out_specs=vmem(len(outs)),
            scratch_shapes=list(scratch),
            compiler_params=pltpu.CompilerParams(vmem_limit_bytes=VMEM_LIMIT),
            name=name,
        )(core, *operands)

    return call


def outputs(layer_output, input_grad, grad_wq, grad_wk, grad_wv, grad_wo, hidden_grads, small):
    model = grad_wq.shape[0]
    base = small.shape[0] - 12
    vector = lambda index: small[index]
    return (
        layer_output,
        input_grad,
        grad_wq.astype(F32),
        vector(base + 6),
        grad_wk.astype(F32),
        grad_wv.astype(F32),
        vector(base + 7),
        grad_wo.astype(F32),
        vector(base + 4),
        vector(base),
        vector(base + 1),
        hidden_grads[:, :model].T,
        small[:base].reshape(-1),
        hidden_grads[:, model:],
        vector(base + 5),
        vector(base + 2),
        vector(base + 3),
    )


def layer_call(tokens, cotangent, segment_ids, mask_positions, vecs, wq, wk, wv, wo, wup, wdown):
    _, stretch, model = tokens.shape
    hidden = wup.shape[1]
    masks = mask_positions.shape[2]
    count, half, full, width = 2 * masks, 2 * stretch, 4 * stretch, model // 2
    units = hidden // 32
    shaped = jax.ShapeDtypeStruct
    low = lambda *shape: pltpu.VMEM(shape, BF16)
    wide = lambda *shape: pltpu.VMEM(shape, F32)
    scratch = [
        low(full, model), low(full, model), low(model, width), low(model, width), low(model, width), low(model, model),
        low(model, hidden), low(hidden, model), low(full, width), low(full, width), low(count, width), low(count, width),
        wide(HEADS // 2, count, full), low(count, model), low(count, full), low(2, masks, width), low(2, masks, model),
        wide(hidden // model, masks, model), low(count, width), low(full, model), low(4, model, width),
        low(4 * units, 2 * model), low(4, units, 2 * model), low(2, 4, masks, model), low(2, 4, masks, model),
        wide(masks, model), wide(7, 16, model), wide(4, 16, model),
        low(full, width), low(full, width), low(half, width), wide(stretch, model), low(stretch, model), low(stretch, model),
        low(half, model), low(half, model), wide(half, model), low(stretch, model), low(stretch, model),
    ]
    for order in ("xyz", "zyx", "xyz", "xyz"):
        size, at = model, 0
        for dim in order:
            ways = 4 if dim == "z" else 2
            size //= ways
            at += size * (ways - 1)
        scratch.append(low(at, width))
    for order in ("xyz", "zyx", "xyz", "xyz"):
        size, at = model, 0
        for dim in order[:2]:
            size //= 4 if dim == "z" else 2
            at += size
        scratch.append(low(at, width))
    scratch += [pltpu.SemaphoreType.DMA((8,)), pltpu.SemaphoreType.DMA((120,)), pltpu.SemaphoreType.DMA((120,))]
    anywhere = [pl.BlockSpec(memory_space=pl.ANY)]
    return pl.pallas_call(
        layer_kernel,
        out_shape=(
            shaped((2, stretch, model), BF16),
            shaped((2, stretch, model), F32),
            shaped((model, model), BF16),
            shaped((model, model), BF16),
            shaped((model, model), BF16),
            shaped((model, model), BF16),
            shaped((units, 2 * model), F32),
            shaped((16, model), F32),
        ),
        in_specs=anywhere * 2 + vmem(3) + anywhere * 6,
        out_specs=vmem(8),
        scratch_shapes=scratch,
        compiler_params=pltpu.CompilerParams(collective_id=0, has_side_effects=True, vmem_limit_bytes=62 * 2**20),
        name="layer",
    )(tokens, cotangent, segment_ids, mask_positions, vecs, wq, wk, wv, wo, wup, wdown)


def on_device(
    rows_total,
    tokens,
    cotangent,
    segment_ids,
    mask_positions,
    query_weight,
    query_bias,
    key_weight,
    value_weight,
    value_bias,
    output_weight,
    output_bias,
    first_gain,
    first_shift,
    up_weight,
    up_bias,
    down_weight,
    down_bias,
    second_gain,
    second_shift,
):
    if rows_total == 8:
        vecs = jnp.concatenate(
            [up_bias]
            + [query_bias, value_bias, output_bias, first_gain, first_shift, down_bias, second_gain, second_shift]
        ).reshape(-1, tokens.shape[2])
        layer_output, input_grad, go, gq, gk, gv, hidden_grads, small = layer_call(
            tokens, cotangent, segment_ids, mask_positions, vecs, query_weight, key_weight, value_weight, output_weight, up_weight, down_weight
        )
        return outputs(layer_output, input_grad, gq, gk, gv, go, hidden_grads, small)
    _, stretch, model = tokens.shape
    hidden = up_weight.shape[1]
    width = model // 2
    heads = HEADS // 2
    masks = mask_positions.shape[2]
    seq = lax.axis_index("seq")
    row = seq // 2
    core = seq % 2
    across = [(i, (i + 2) % 4) for i in range(4)]
    beside = [(i, i + 1 - 2 * (i % 2)) for i in range(4)]

    def swap(value):
        return lax.ppermute(value, "seq", across)

    def trade(value):
        return lax.ppermute(value, "seq", beside)

    def take(array, index):
        return lax.dynamic_index_in_dim(array, index, 0, keepdims=False)

    half = jnp.concatenate([take(tokens, row), swap(take(tokens, 1 - row))], axis=0)
    peer = trade(half)
    cot_half = jnp.concatenate([take(cotangent, row), swap(take(cotangent, 1 - row))], axis=0)
    cot_peer = trade(cot_half)
    blocks = jnp.stack([2 * row + core, 2 * (1 - row) + core, 2 * row + 1 - core, 2 * (1 - row) + 1 - core])
    positions = (blocks[:, None] * stretch + jnp.arange(stretch, dtype=jnp.int32)[None, :]).reshape(-1)
    segments = jnp.take(take(segment_ids, row).reshape(4, stretch), blocks, axis=0).reshape(-1)
    slots = take(mask_positions, row).reshape(-1)
    pos, seg, slot_col = positions[None, :], segments[None, :], slots[:, None]
    pos_col, seg_col, slot_row = positions[:, None], segments[:, None], slots[None, :]
    core_scalar = core.reshape(1).astype(jnp.int32)
    line = lambda value: value.reshape(1, -1)
    full = 4 * stretch
    count = 2 * masks
    shaped = jax.ShapeDtypeStruct

    keys, values, queries, context, probs, picked = local_call(
        project_kernel,
        (
            shaped((full, width), BF16),
            shaped((full, width), BF16),
            shaped((count, width), BF16),
            shaped((count, width), BF16),
            shaped((heads, count, full), F32),
            shaped((count, model), BF16),
        ),
        "project",
    )(core_scalar, half, peer, pos, seg, slot_col, query_weight, line(query_bias), key_weight, value_weight, line(value_bias))

    two = context.reshape(2, masks, width)
    ctx_peer = trade(take(two, 1 - core))
    normed_low, feed, branch_low, grad_h1, small = local_call(
        masked_kernel,
        (
            shaped((masks, model), BF16),
            shaped((masks, model), BF16),
            shaped((masks, model), BF16),
            shaped((masks, model), F32),
            shaped((16, model), F32),
        ),
        "masked",
    )(
        core_scalar, take(two, core), ctx_peer, picked, cot_half, cot_peer, pos, slot_col, output_weight, line(output_bias),
        line(first_gain), line(first_shift), up_weight, line(up_bias), down_weight, line(down_bias), line(second_gain), line(second_shift),
    )
    branch_peer = trade(branch_low)
    grads, igrad_own, igrad_peer, bias = local_call(
        back_kernel,
        (
            shaped((4, model, width), BF16),
            shaped((2 * stretch, model), F32),
            shaped((2 * stretch, model), BF16),
            shaped((2, width), F32),
        ),
        "back",
        [pltpu.VMEM((count, width), BF16), pltpu.VMEM((full, width), BF16), pltpu.VMEM((full, width), BF16)],
    )(
        core_scalar, keys, values, queries, context, probs, picked, branch_low, branch_peer, grad_h1, half, peer, pos_col, slot_row,
        query_weight, key_weight, value_weight, output_weight,
    )
    igrad = igrad_own + trade(igrad_peer).astype(F32)
    igrad_other = swap(igrad[stretch:].astype(BF16)).astype(F32)
    igrad_mine = igrad[:stretch]
    input_grad = jnp.where(row == 0, jnp.stack([igrad_mine, igrad_other]), jnp.stack([igrad_other, igrad_mine]))

    ctx_own, ctx_other = local_call(
        attend_kernel, (shaped((2 * stretch, width), BF16), shaped((2 * stretch, width), BF16)), "attend"
    )(core_scalar, half, peer, seg, seg_col, keys, values, query_weight, line(query_bias))
    out_mine, out_other = local_call(
        feed_kernel, (shaped((stretch, model), BF16), shaped((stretch, model), BF16)), "feed"
    )(
        core_scalar, ctx_own, trade(ctx_other), half, output_weight, line(output_bias), line(first_gain), line(first_shift),
        up_weight, line(up_bias), down_weight, line(down_bias), line(second_gain), line(second_shift),
    )
    out_other = swap(out_other)
    layer_output = jnp.where(row == 0, jnp.stack([out_mine, out_other]), jnp.stack([out_other, out_mine]))

    wide = jnp.zeros((2, model), F32)
    bias_rows = lax.dynamic_update_slice(wide, bias, (0, core * width))
    base = hidden // model + 6
    small = jnp.concatenate([small[:base], bias_rows, small[base + 2 :]], axis=0)

    both = ("rows", "seq")
    small = lax.psum(small, both)
    zero = jnp.zeros((model, model), F32)
    wide_grads = [lax.dynamic_update_slice(zero, grads[k].astype(F32), (0, core * width)) for k in (1, 2, 3)]
    rows_wo = grads[0].reshape(2, width, width).transpose(1, 0, 2).reshape(width, model).astype(F32)
    wide_grads.append(lax.dynamic_update_slice(zero, rows_wo, (core * width, 0)))
    grad_wq, grad_wk, grad_wv, grad_wo = lax.psum(tuple(wide_grads), both)
    pieces = []
    units = hidden // 8
    for part in range(8):
        (piece,) = local_call(hidden_kernel, (shaped((units, 2 * model), BF16),), "hidden")(
            jnp.full((1,), part, jnp.int32), normed_low, feed, up_weight, line(up_bias), down_weight
        )
        pieces.append(piece.astype(F32))
    hidden_grads = lax.psum_scatter(jnp.concatenate(pieces, axis=0), both, scatter_dimension=0, tiled=True)

    return outputs(layer_output, input_grad, grad_wq, grad_wk, grad_wv, grad_wo, hidden_grads, small)


def solution(mesh):
    split = P("rows", "seq", None)
    in_specs = (split, split, P("rows", None), P("rows", None, None)) + (P(),) * 15
    out_specs = (split, split) + (P(),) * 9 + (P(None, ("rows", "seq")), P(), P(("rows", "seq"), None), P(), P(), P())
    return jax.shard_map(
        functools.partial(on_device, mesh.shape["rows"]), mesh=mesh, in_specs=in_specs, out_specs=out_specs, check_vma=False
    )
```

profile of v0, /device:TPU:9, one launch (start us, length us, event | category | flops | bytes accessed | tf_op | source)
XLA Modules:
  0.0 148.7 jit_solution(16826452989775148925)
XLA Ops:
  0.7 0.7 constant_dynamic-update-slice_fusion.8
  1.4 0.7 constant_dynamic-update-slice_fusion.7
  2.1 0.7 constant_dynamic-update-slice_fusion.6
  2.7 0.7 constant_dynamic-update-slice_fusion.5
  3.4 0.7 constant_dynamic-update-slice_fusion.4
  4.1 0.7 constant_dynamic-update-slice_fusion.3
  4.8 0.7 constant_dynamic-update-slice_fusion.2
  5.5 0.7 constant_dynamic-update-slice_fusion.1
  6.2 0.7 constant_dynamic-update-slice_fusion
  6.9 0.6 reshape.40.vecs
  7.5 126.7 %layer.1 = (bf16[2,256,768]{2,1,0:T(8,128)(2,1)}, f32[2,256,768]{2,1,0:T(8,128)}, bf16[768,768]{1,0:T(8,128)(2,1)}, bf16[768,768]{1,0:T(8,128)(2,1)}, bf16[768,7...) custom-call(bf16[2,256,768]{2,1,0:T(8,128)(2,1)} %tokens.1, ...), custom_call_target="tpu_custom_call" | custom-call | tf_op jit(solution)/shard_map/layer/pallas_call | solution.py:907
  134.3 0.0 copy-start.4
  134.3 0.8 slice.39
  135.1 1.6 %slice_reduce_fusion = (f32[768]{0:T(1024)}, f32[768]{0:T(1024)}, f32[768]{0:T(1024)}, f32[768]{0:T(1024)}, f32[768]{0:T(1024)}, /*index=5*/f32[768]{0:T(1024)}, f32[768]{0:T(1024)}, f32[768]{0:T(1024)}) fusion(f32[16,768]{1,0:T(8,128)} %get-tuple-element.28), kind=kLoop, calls=%fused_computation.10 | loop fusion | bytes 49152 | tf_op jit(solution)/shard_map/slice | solution.py:851
  136.8 0.6 reshape.41
  137.4 1.9 %fusion = (f32[96,768]{1,0:T(8,128)}, f32[768,96]{0,1:T(8,128)}) fusion(f32[96,1536]{1,0:T(8,128)} %get-tuple-element.32), kind=kLoop, calls=%fused_computation.18 | loop fusion | bytes 1179648 | tf_op jit(solution)/shard_map/slice | solution.py:866
  139.3 0.0 copy-done.4
  139.3 0.0 copy-start.3
  139.3 1.6 %convert_element_type.12 = f32[768,768]{1,0:T(8,128)} convert(bf16[768,768]{1,0:T(8,128)(2,1)S(1)} %copy-done.4) | non-fusion elementwise | flops 589824 | bytes 3538944 | tf_op jit(solution)/shard_map/convert_element_type | solution.py:855
  140.9 0.1 copy-done.3
  140.9 0.0 copy-start.2
  141.0 1.6 %convert_element_type.13 = f32[768,768]{1,0:T(8,128)} convert(bf16[768,768]{1,0:T(8,128)(2,1)S(1)} %copy-done.3) | non-fusion elementwise | flops 589824 | bytes 3538944 | tf_op jit(solution)/shard_map/convert_element_type | solution.py:857
  142.5 0.1 copy-done.2
  142.6 0.0 copy-start.1
  142.6 1.6 %convert_element_type.14 = f32[768,768]{1,0:T(8,128)} convert(bf16[768,768]{1,0:T(8,128)(2,1)S(1)} %copy-done.2) | non-fusion elementwise | flops 589824 | bytes 3538944 | tf_op jit(solution)/shard_map/convert_element_type | solution.py:858
  144.2 0.1 copy-done.1
  144.3 0.0 copy-start.5
  144.3 1.6 %convert_element_type.15 = f32[768,768]{1,0:T(8,128)} convert(bf16[768,768]{1,0:T(8,128)(2,1)S(1)} %copy-done.1) | non-fusion elementwise | flops 589824 | bytes 3538944 | tf_op jit(solution)/shard_map/convert_element_type | solution.py:860
  145.9 0.0 copy-done.5
  145.9 0.9 copy.46
  146.8 0.8 copy-done
  147.6 1.1 copy.47
  (1 shorter events, 0.0 us)
Async XLA Ops:
  134.3 5.0 %copy-start.4 = (bf16[768,768]{1,0:T(8,128)(2,1)S(1)}, bf16[768,768]{1,0:T(8,128)(2,1)}, u32[]{:S(2)}) copy-start(bf16[768,768]{1,0:T(8,128)(2,1)} %get-tuple-element.27) | copy-start | bytes 3538948
  139.3 1.7 %copy-start.3 = (bf16[768,768]{1,0:T(8,128)(2,1)S(1)}, bf16[768,768]{1,0:T(8,128)(2,1)}, u32[]{:S(2)}) copy-start(bf16[768,768]{1,0:T(8,128)(2,1)} %get-tuple-element.29) | copy-start | bytes 3538948
  140.9 1.7 %copy-start.2 = (bf16[768,768]{1,0:T(8,128)(2,1)S(1)}, bf16[768,768]{1,0:T(8,128)(2,1)}, u32[]{:S(2)}) copy-start(bf16[768,768]{1,0:T(8,128)(2,1)} %get-tuple-element.30) | copy-start | bytes 3538948
  142.6 1.7 %copy-start.1 = (bf16[768,768]{1,0:T(8,128)(2,1)S(1)}, bf16[768,768]{1,0:T(8,128)(2,1)}, u32[]{:S(2)}) copy-start(bf16[768,768]{1,0:T(8,128)(2,1)} %get-tuple-element.31) | copy-start | bytes 3538948
  144.3 1.6 %copy-start.5 = (bf16[2,256,768]{2,1,0:T(8,128)(2,1)S(1)}, bf16[2,256,768]{2,1,0:T(8,128)(2,1)}, u32[]{:S(2)}) copy-start(bf16[2,256,768]{2,1,0:T(8,128)(2,1)} %get-tuple-element.60) | copy-start | bytes 2359300
  145.9 1.7 %copy-start = (f32[2,256,768]{2,1,0:T(8,128)S(1)}, f32[2,256,768]{2,1,0:T(8,128)}, u32[]{:S(2)}) copy-start(f32[2,256,768]{2,1,0:T(8,128)} %get-tuple-element.61) | copy-start | bytes 4718596
where the time goes:
time: 150 us; the launch traced here: 149 us
  Pallas kernels  127 us (85%)
  local copies, waits for them, and re-layouts  15 us (10%)
  other arithmetic  6.3 us (4%)
    pallas_call x1, Pallas kernels, layer_call(): pl.pallas_call(layer_kernel, out_shape=(shaped((2, stretch, model), BF16)...  127 us
    unnamed x22, local copies, waits for them, and re-layouts  8.69 us

commit v1 on v0

--- a/solution.py
+++ b/solution.py
@@ -14,6 +14,32 @@
 BF16 = jnp.bfloat16
 MESH = pl.DeviceIdType.MESH
 VMEM_LIMIT = 56 * 2**20
+ORDERS = ("xyz", "zxy", "xyz", "yxz")
+PLAN = {
+    "G0": ("Sr00",),
+    "G23": ("Sr30",),
+    "G1": ("Sr20", "Sr10"),
+    "dx": ("Er00", "Ss0"),
+    "a1": ("Es0", "Ss1", "Sr01"),
+    "a2": ("Ed", "Er20", "Er30", "Sr31"),
+    "a4": ("Es1", "Ss2", "Sr21"),
+    "a5": ("Er01", "Sr02", "Ef"),
+    "a6": ("Es2", "Si", "Ss3", "Er10", "Sr11", "Er31"),
+    "a7": ("Er21", "EH", "Er11", "Sr22", "Er02"),
+    "a8": ("Es3",),
+    "a9": ("Sr32",),
+    "a10": ("Er22", "Sr12"),
+    "a11": ("Ei", "Sg22"),
+    "f0": ("Er12", "Sg12", "Er32"),
+    "f1": ("Sg32",),
+    "f2": ("Eg12", "Sg11", "Eg22", "Sg21"),
+    "f3": ("Sg02",),
+    "f4": ("Eg11", "Eg32", "Sg31"),
+    "f5": ("Sg10",),
+    "f6": ("Eg02", "Sg01"),
+    "f7": ("Eg21", "Sg20", "Eg31", "Eh"),
+    "end": ("Sg30", "Eg01", "Sg00", "So", "Eg20", "St2", "Eg30", "St3", "Et2", "Eg10", "St1", "Et3", "Et1", "Eg00", "St0", "Et0", "Eo"),
+}
 
 
 def dot(left, right):
@@ -273,12 +299,13 @@
 
 
 def layer_kernel(
-    tokens, cotangent, segments, slots, vecs, wq, wk, wv, wo, wup, wdown,
-    layer_out, input_grad, out_o, out_q, out_k, out_v, hidden_out, small_out,
+    tokens, cotangent, segments_in, slots_in, up_bias_in, bq_in, bv_in, bo_in, g1_in, s1_in, bdown_in, g2_in, s2_in, wq, wk, wv, wo, wup, wdown,
+    layer_out, input_grad, out_o, out_q, out_k, out_v, up_out, down_out, small_out,
+    segments, slots, up_bias, bq, bv, bo, g1, s1, bdown, g2, s2, vecs, wq_t, wkv_t, wo_t, keys_t, values_t,
     xs, cs, wq_v, wk_v, wv_v, wo_v, wup_v, wdown_v, keys, values, queries, context, probs, picked, chosen, ctx_both, gb_both,
     slopes, dq_low, dkv_low, grads, hidden_grads, hidden_in, fac_normed, fac_feed, grad_h1, small_in, small_z,
-    all_queries, all_context, ctx_in, total, y1_keep, out_send, dx_send, dx_in, dx_own, igrad_send, igrad_in,
-    in_o, in_q, in_k, in_v, mid_o, mid_q, mid_k, mid_v, local_sem, send_sem, recv_sem,
+    all_queries, all_context, ctx_in, total, y1_keep, out_send, igrad_send, igrad_in,
+    in_o, in_q, in_k, in_v, local_sem, send_sem, recv_sem,
 ):
     z, x, y, core = place_here()
     row = y
@@ -290,7 +317,7 @@
     count = 2 * masks
     hidden = wup.shape[1]
     parts = hidden // model
-    units = hidden_out.shape[0]
+    units = down_out.shape[0]
     others = [(z + k) % 4 for k in (1, 2, 3)]
     at_y, at_x, twin = device(z, x, 1 - y, core), device(z, 1 - x, y, core), device(z, x, y, 1 - core)
     columns = [device(o, x, y, core) for o in others]
@@ -322,39 +349,50 @@
     def half_vector(index):
         return vecs[index : index + 1, mine]
 
+    small_pairs = (
+        (segments_in, segments), (slots_in, slots), (up_bias_in, up_bias), (bq_in, bq), (bv_in, bv), (bo_in, bo), (g1_in, g1),
+        (s1_in, s1), (bdown_in, bdown), (g2_in, g2), (s2_in, s2),
+    )
     own_tokens = local(tokens.at[row], xs.at[pl.ds(0, stretch)], 0)
     get_wk = local(wk.at[:, mine], wk_v, 1)
     get_wv = local(wv.at[:, mine], wv_v, 2)
+    get_small = [local(src, dst, 8 + k) for k, (src, dst) in enumerate(small_pairs)]
     get_wq = local(wq.at[:, mine], wq_v, 3)
     own_cot = local(cotangent.at[row], cs.at[pl.ds(0, stretch)], 4)
     get_wo = local(wo, wo_v, 5)
     get_up = local(wup, wup_v, 6)
     get_down = local(wdown, wdown_v, 7)
 
+    near = [(1 - x, y), (x, 1 - y), (1 - x, 1 - y)]
+    greeted = [twin] + columns + [device(z, nx, ny, c) for nx, ny in near for c in range(2)]
     barrier = pltpu.get_barrier_semaphore()
-    for cx in range(2):
-        for cy in range(2):
-            for cc in range(2):
-                @pl.when(jnp.logical_not((cx == x) & (cy == y) & (cc == core)))
-                def _(cx=cx, cy=cy, cc=cc):
-                    pl.semaphore_signal(barrier, inc=1, device_id=device(z, cx, cy, cc), device_id_type=MESH)
-    for target in columns:
+    for target in greeted:
         pl.semaphore_signal(barrier, inc=1, device_id=target, device_id_type=MESH)
-    pl.semaphore_wait(barrier, 10)
+    pl.semaphore_wait(barrier, len(greeted))
 
     piece = stretch // 2
     tok_y = [
         push(tokens.at[1 - row, pl.ds(k * piece, piece)], xs.at[pl.ds(stretch + k * piece, piece)], k, at_y) for k in range(2)
     ]
     tok_c = push(tokens.at[row], xs.at[pl.ds(half, stretch)], 2, twin)
-    cot_y = push(cotangent.at[1 - row], cs.at[pl.ds(stretch, stretch)], 3, at_y)
     cot_c = push(cotangent.at[row], cs.at[pl.ds(half, stretch)], 4, twin)
+
+    for copy in get_small:
+        copy.wait()
+    for part in range(parts):
+        vecs[part : part + 1, :] = up_bias[part * model : (part + 1) * model].reshape(1, model)
+    for place, value in enumerate((bq, bv, bo, g1, s1, bdown, g2, s2)):
+        vecs[parts + place : parts + place + 1, :] = value[...].reshape(1, model)
 
     def key_values(start):
         here = pl.ds(start, stretch)
         block = xs[here, :]
-        keys[here, :] = dot(block, wk_v[...]).astype(BF16)
-        values[here, :] = (dot(block, wv_v[...]) + half_vector(5)).astype(BF16)
+        block_keys = dot(block, wk_v[...]).astype(BF16)
+        block_values = (dot(block, wv_v[...]) + half_vector(5)).astype(BF16)
+        keys[here, :] = block_keys
+        values[here, :] = block_values
+        keys_t[:, here] = block_keys.T
+        values_t[:, here] = block_values.T
 
     blocks = [2 * y + core, 2 * (1 - y) + core, 2 * y + 1 - core, 2 * (1 - y) + 1 - core]
     lane = lax.broadcasted_iota(jnp.int32, (1, stretch), 1)
@@ -375,11 +413,16 @@
     key_values(0)
     tok_c.wait_recv()
     key_values(half)
+    get_wq.wait()
+    wkv_t[:width, :] = wk_v[...].T
+    wkv_t[width:, :] = wv_v[...].T
+    wq_t[...] = wq_v[...].T
     forward = []
     for k in range(2):
         tok_y[k].wait_recv()
         src = xs.at[pl.ds(stretch + k * piece, piece)]
         forward.append(push(src, xs.at[pl.ds(half + stretch + k * piece, piece)], 5 + k, twin))
+    cot_y = push(cotangent.at[1 - row], cs.at[pl.ds(stretch, stretch)], 3, at_y)
     key_values(stretch)
     for copy in forward:
         copy.wait_recv()
@@ -387,7 +430,6 @@
 
     rows = dot(chosen[...], xs[...]).astype(BF16)
     picked[...] = rows
-    get_wq.wait()
     queries[...] = (dot(rows, wq_v[...]) + half_vector(4)).astype(BF16)
     sequence = lax.broadcasted_iota(jnp.int32, (count, 1), 0) // masks
     same = seg_row == sequence.astype(F32)
@@ -395,12 +437,12 @@
     for pair in range(pairs):
         lanes = slice(pair * 128, pair * 128 + 128)
         pair_queries = queries[:, lanes].astype(F32) * 0.125
-        pair_keys, pair_values = keys[:, lanes], values[:, lanes]
+        pair_keys, pair_values = keys_t[lanes, :], values[:, lanes]
         outs = []
         for side in range(2):
             keep = lane_is((count, 128), side * 64, side * 64 + 64)
             head_queries = jnp.where(keep, pair_queries, 0.0).astype(BF16)
-            scores = jnp.where(same, dot_nt(head_queries, pair_keys), MASKED_SCORE)
+            scores = jnp.where(same, dot(head_queries, pair_keys), MASKED_SCORE)
             weights = jnp.exp(scores - jnp.max(scores, axis=-1, keepdims=True))
             share = weights / jnp.sum(weights, axis=-1, keepdims=True)
             probs[pair * 2 + side] = share
@@ -417,6 +459,7 @@
         value = (dot(xs[start : start + stretch, :], wq_v[...]) + half_vector(4)).astype(BF16)
         all_queries[start : start + stretch, :] = (value.astype(F32) * 0.125).astype(BF16)
     get_wo.wait()
+    wo_t[...] = wo_v[mine, :].T
     ctx_c.wait_recv()
 
     branch = dot(ctx_both[0], wo_v[:width, :]) + dot(ctx_both[1], wo_v[width:, :]) + vector(6)
@@ -443,13 +486,15 @@
     fac_feed[core, z] = gf
     spot = fac_feed.at[core, z]
     feed_z = [push(spot, spot, 12 + k, columns[k]) for k in range(3)]
-    gy1 = gh2
+    gf_t = gf.T
+    gy1_t = jnp.zeros((model, masks), F32)
     small_in[0] = jnp.zeros(small_in.shape[1:], F32)
     for part in range(parts):
         there = slice(part * model, (part + 1) * model)
-        gp = (dot_nt(gf, wdown_v[there, :]) * slopes[part]).astype(BF16)
+        gp = (dot(wdown_v[there, :], gf_t).T * slopes[part]).astype(BF16)
         small_in[0, part : part + 1, :] = jnp.sum(gp.astype(F32), axis=0, keepdims=True)
-        gy1 = gy1 + dot_nt(gp, wup_v[:, there])
+        gy1_t = gy1_t + dot(wup_v[:, there], gp.T)
+    gy1 = gh2 + gy1_t.T
     gh1 = norm_back(gy1, n1, r1, vector(7))
     grad_h1[...] = gh1
     gb = gh1.astype(BF16)
@@ -462,9 +507,8 @@
     spots = {"x": x, "y": y, "z": z}
     sizes = {"x": 2, "y": 2, "z": 4}
     dims = {"x": [at_x], "y": [at_y], "z": columns}
-    orders = ["xyz", "zyx", "xyz", "xyz"]
+    orders = ORDERS
     ins = [in_o, in_q, in_k, in_v]
-    mids = [mid_o, mid_q, mid_k, mid_v]
     outs = [out_o, out_q, out_k, out_v]
 
     def regions(job):
@@ -482,13 +526,6 @@
             at += size * (sizes[dim] - 1)
         return at, size // sizes[orders[job][stage]]
 
-    def mid_place(job, stage):
-        at, size = 0, model
-        for dim in orders[job][:stage]:
-            size = size // sizes[dim]
-            at += size
-        return at
-
     def out_at(job, base, size):
         if job == 0:
             side = base // width
@@ -500,13 +537,11 @@
     def reduce_copies(job, stage):
         dim = orders[job][stage]
         at, size = in_place(job, stage)
+        base, _ = regions(job)[stage]
         copies = []
         for k, target in enumerate(dims[dim]):
             other = (spots[dim] + k + 1) % sizes[dim]
-            if stage == 0:
-                src = grads.at[job, pl.ds(pl.multiple_of(other * size, 16), size)]
-            else:
-                src = mids[job].at[pl.ds(pl.multiple_of(mid_place(job, stage - 1) + other * size, 16), size)]
+            src = grads.at[job, pl.ds(pl.multiple_of(base + other * size, 16), size)]
             dst = ins[job].at[pl.ds(at + k * size, size)]
             copies.append(remote(src, dst, 40 + job * 20 + stage * 3 + k, target))
         return copies
@@ -520,21 +555,16 @@
             copy.wait()
         dim = orders[job][stage]
         at, size = in_place(job, stage)
-        here = spots[dim] * size
-        if stage == 0:
-            value = grads[job, pl.ds(pl.multiple_of(here, 16), size)].astype(F32)
-        else:
-            value = mids[job][pl.ds(pl.multiple_of(mid_place(job, stage - 1) + here, 16), size)].astype(F32)
+        base, _ = regions(job)[stage + 1]
+        here = pl.ds(pl.multiple_of(base, 16), size)
+        value = grads[job, here].astype(F32)
         for k in range(len(dims[dim])):
             value = value + ins[job][pl.ds(at + k * size, size)].astype(F32)
         value = value.astype(BF16)
         if stage < 2:
-            mids[job][pl.ds(mid_place(job, stage), size)] = value
-            reduce_start(job, stage + 1)
+            grads[job, here] = value
         else:
-            base, _ = regions(job)[3]
             out_at(job, base, size)[...] = value
-            gather_start(job, 2)
 
     def gather_copies(job, stage):
         base, size = regions(job)[stage + 1]
@@ -555,10 +585,6 @@
     def gather_end(job, stage):
         for copy in gather_copies(job, stage):
             copy.wait()
-        if stage > 0:
-            gather_start(job, stage - 1)
-        else:
-            twin_copy(job).start()
 
     def small_copies(stage):
         if stage < 3:
@@ -577,7 +603,6 @@
             small_in[2 * stage + 2] = small_in[2 * stage] + small_in[2 * stage + 1]
             if stage == 2:
                 small_z[z] = small_in[6]
-            small_start(stage + 1)
         else:
             small_out[...] = (small_z[0] + small_z[1]) + (small_z[2] + small_z[3])
 
@@ -642,24 +667,67 @@
         value = hidden_in[0].astype(F32)
         for k in range(1, 4):
             value = value + hidden_in[k].astype(F32)
-        hidden_out[...] = value
+        up_out[...] = value[:, :model]
+        down_out[...] = value[:, model:]
+
+    def igrad_copy():
+        return remote(igrad_send, igrad_in, 29, at_y)
+
+    def igrad_step():
+        remote(cs.at[pl.ds(0, half)], cs.at[pl.ds(half, half)], 28, twin).wait_recv()
+        input_grad[row] = input_grad[row] + cs[half : half + stretch, :].astype(F32)
+        igrad_send[...] = (input_grad[1 - row] + cs[half + stretch :, :].astype(F32)).astype(BF16)
+
+    def igrad_end():
+        igrad_copy().wait()
+        input_grad[1 - row] = igrad_in[...].astype(F32)
+
+    def out_copy():
+        return remote(out_send, layer_out.at[row], 31, at_y)
+
+    def act(name):
+        start, kind, rest = name[0] == "S", name[1], [int(c) for c in name[2:]]
+        if kind == "r":
+            (reduce_start if start else reduce_end)(*rest)
+        elif kind == "g":
+            (gather_start if start else gather_end)(*rest)
+        elif kind == "t":
+            twin_copy(*rest).start() if start else twin_copy(*rest).wait()
+        elif kind == "s":
+            (small_start if start else small_end)(*rest)
+        elif kind == "d":
+            igrad_step()
+        elif kind == "i":
+            igrad_copy().start() if start else igrad_end()
+        elif kind == "o":
+            out_copy().start() if start else out_copy().wait()
+        elif kind == "f":
+            factors_on()
+        elif kind == "H":
+            hidden_make()
+        elif kind == "h":
+            hidden_end()
+
+    def act_on(name):
+        for each in PLAN.get(name, ()):
+            act(each)
 
     gb = gb_both[...].reshape(count, model)
-    gctx = dot_nt(gb, wo_v[mine, :]).astype(BF16)
+    gctx = dot(gb, wo_t[...]).astype(BF16)
     value = dot_tn(context[...], gb).astype(BF16)
     grads[0, :width, :] = value[:, :width]
     grads[0, width:, :] = value[:, width:]
-    reduce_start(0, 0)
+    act_on("G0")
     for pair in range(pairs):
         lanes = slice(pair * 128, pair * 128 + 128)
-        pair_keys, pair_values, pair_queries = keys[:, lanes], values[:, lanes], queries[:, lanes]
+        pair_keys, pair_values, pair_queries = keys[:, lanes], values_t[lanes, :], queries[:, lanes]
         pair_gctx = gctx[:, lanes]
         dqs, dks, dvs = [], [], []
         for side in range(2):
             keep = lane_is((count, 128), side * 64, side * 64 + 64)
             head_gctx = jnp.where(keep, pair_gctx.astype(F32), 0.0).astype(BF16)
             share = probs[pair * 2 + side]
-            gp = dot_nt(head_gctx, pair_values)
+            gp = dot(head_gctx, pair_values)
             spread = jnp.sum(share * gp, axis=-1, keepdims=True)
             gs = (share * (gp - spread)).astype(BF16)
             dqs.append(dot(gs, pair_keys))
@@ -670,82 +738,48 @@
         first = lane_is((full, 128), 0, 64)
         dkv_low[:, lanes] = (jnp.where(first, dks[0], dks[1]) * 0.125).astype(BF16)
         dkv_low[:, width + pair * 128 : width + pair * 128 + 128] = jnp.where(first, dvs[0], dvs[1]).astype(BF16)
-        if pair == 0:
-            factors_on()
-        if pair == 1:
-            reduce_end(0, 0)
+    act_on("heads")
     for start in range(0, model, 256):
         value = dot_tn(xs[:, start : start + 256], dkv_low[...]).astype(BF16)
         grads[2, start : start + 256, :] = value[:, :width]
         grads[3, start : start + 256, :] = value[:, width:]
-    reduce_start(2, 0)
-    reduce_start(3, 0)
+    act_on("G23")
     grads[1] = dot_tn(picked[...], dq_low[...]).astype(BF16)
-    reduce_start(1, 0)
-    reduce_end(0, 1)
+    act_on("G1")
     small_in[0, parts + 6 : parts + 7, mine] = jnp.sum(dq_low[...].astype(F32), axis=0, keepdims=True)
     small_in[0, parts + 7 : parts + 8, mine] = jnp.sum(dkv_low[:, width:].astype(F32), axis=0, keepdims=True)
-    small_start(0)
-
-    spread_rows = dot_nt(dq_low[...], wq_v[...])
+
+    spread_rows = dot(dq_low[...], wq_t[...])
     zero = jnp.zeros((masks, model), F32)
     is_first = core == 0
     gh1 = grad_h1[...]
     spread_rows = spread_rows + jnp.concatenate([jnp.where(is_first, gh1, zero), jnp.where(is_first, zero, gh1)], axis=0)
     high = spread_rows.astype(BF16)
     rest = (spread_rows - high.astype(F32)).astype(BF16)
-    dx_c = None
+    cot_f.wait_send()
+    pending[:] = [copy for copy in pending if copy is not cot_f]
     for start in (half, half + stretch, 0, stretch):
         here = slice(start, start + stretch)
         value = dot_tn(chosen[:, here], high) + dot_tn(chosen[:, here], rest)
-        value = value + dot_nt(dkv_low[here, :width], wk_v[...]) + dot_nt(dkv_low[here, width:], wv_v[...])
+        value = value + dot(dkv_low[here, :], wkv_t[...])
         if start < half:
-            dx_own[here, :] = value
+            input_grad[row if start == 0 else 1 - row] = value
         else:
-            dx_send[start - half : start - half + stretch, :] = value.astype(BF16)
+            cs[start - half : start - half + stretch, :] = value.astype(BF16)
             if start > half:
-                dx_c = push(dx_send, dx_in, 28, twin)
-
-    igrad_copy = remote(igrad_send, igrad_in, 29, at_y)
-
-    def igrad_step():
-        dx_c.wait_recv()
-        input_grad[row] = dx_own[:stretch, :] + dx_in[:stretch, :].astype(F32)
-        igrad_send[...] = (dx_own[stretch:, :] + dx_in[stretch:, :].astype(F32)).astype(BF16)
-        remote(igrad_send, igrad_in, 29, at_y).start()
-
-    hidden_make()
-
-    def hooks(step, table):
-        for at, actions in table.items():
-            @pl.when(step == at)
-            def _(actions=actions):
-                for action in actions:
-                    action[0](*action[1:])
+                push(cs.at[pl.ds(0, half)], cs.at[pl.ds(half, half)], 28, twin)
+
+    act_on("dx")
+
+    def hooks(step, prefix, count):
+        for at in range(count):
+            if prefix + str(at) in PLAN:
+                @pl.when(step == at)
+                def _(at=at):
+                    act_on(prefix + str(at))
 
     def ctx_copy():
         return remote(all_context.at[pl.ds(half, half)], ctx_in, 30, twin)
-
-    attend_table = {
-        0: [(reduce_end, 2, 0), (small_end, 0)],
-        1: [(reduce_end, 1, 0), (igrad_step,)],
-        2: [(reduce_end, 0, 2), (small_end, 1)],
-        3: [(reduce_end, 3, 0), (reduce_end, 2, 1)],
-        4: [(gather_end, 0, 2), (reduce_end, 1, 1)],
-        5: [(reduce_end, 2, 2), (small_end, 2)],
-        6: [(reduce_end, 3, 1), (gather_end, 0, 1)],
-        7: [(reduce_end, 1, 2), (gather_end, 2, 2)],
-        8: [(reduce_end, 3, 2), (small_end, 3)],
-        9: [(gather_end, 2, 1), (gather_end, 1, 2)],
-        10: [(gather_end, 3, 2)],
-        11: [(gather_end, 0, 0), (gather_end, 1, 1)],
-    }
-    feed_table = {
-        1: [(gather_end, 3, 1)],
-        3: [(gather_end, 2, 0)],
-        5: [(gather_end, 1, 0)],
-        6: [(hidden_end,)],
-    }
 
     def attend_step(step, carry):
         tile, pair = (step // pairs + 2) % 4, step % pairs
@@ -756,12 +790,12 @@
         seg_col = jnp.where(place.astype(F32) >= split, 1.0, 0.0)
         same_here = seg_col == seg_row
         pair_queries = all_queries[here, lanes].astype(F32)
-        pair_keys, pair_values = keys[:, lanes], values[:, lanes]
+        pair_keys, pair_values = keys_t[lanes, :], values[:, lanes]
         found = []
         for side in range(2):
             keep = lane_is((stretch, 128), side * 64, side * 64 + 64)
             head_queries = jnp.where(keep, pair_queries, 0.0).astype(BF16)
-            scores = jnp.where(same_here, dot_nt(head_queries, pair_keys), MASKED_SCORE)
+            scores = jnp.where(same_here, dot(head_queries, pair_keys), MASKED_SCORE)
             weights = jnp.exp(scores - jnp.max(scores, axis=-1, keepdims=True))
             found.append(dot(weights.astype(BF16), pair_values) / jnp.sum(weights, axis=-1, keepdims=True))
         first = lane_is((stretch, 128), 0, 64)
@@ -771,14 +805,11 @@
         def _():
             ctx_copy().start()
 
-        hooks(step, attend_table)
+        hooks(step, "a", 4 * pairs)
         return carry
 
     lax.fori_loop(0, 4 * pairs, attend_step, 0)
     ctx_copy().wait()
-
-    def out_copy():
-        return remote(out_send, layer_out.at[row], 31, at_y)
 
     def feed_step(step, carry):
         tile, part = 1 - step // parts, step % parts
@@ -806,22 +837,16 @@
             @pl.when(tile == 1)
             def _():
                 out_send[...] = value
-                out_copy().start()
 
             @pl.when(tile == 0)
             def _():
                 layer_out[row] = value
 
-        hooks(step, feed_table)
+        hooks(step, "f", 2 * parts)
         return carry
 
     lax.fori_loop(0, 2 * parts, feed_step, 0)
-    gather_end(3, 0)
-    igrad_copy.wait()
-    input_grad[1 - row] = igrad_in[...].astype(F32)
-    out_copy().wait()
-    for job in range(4):
-        twin_copy(job).wait()
+    act_on("end")
     for copy in pending:
         copy.wait_send()
 
@@ -845,7 +870,7 @@
     return call
 
 
-def outputs(layer_output, input_grad, grad_wq, grad_wk, grad_wv, grad_wo, hidden_grads, small):
+def outputs(layer_output, input_grad, grad_wq, grad_wk, grad_wv, grad_wo, up_part, down_part, small):
     model = grad_wq.shape[0]
     base = small.shape[0] - 12
     vector = lambda index: small[index]
@@ -861,25 +886,27 @@
         vector(base + 4),
         vector(base),
         vector(base + 1),
-        hidden_grads[:, :model].T,
+        up_part.T,
         small[:base].reshape(-1),
-        hidden_grads[:, model:],
+        down_part,
         vector(base + 5),
         vector(base + 2),
         vector(base + 3),
     )
 
 
-def layer_call(tokens, cotangent, segment_ids, mask_positions, vecs, wq, wk, wv, wo, wup, wdown):
+def layer_call(tokens, cotangent, segment_ids, mask_positions, vectors, weights):
     _, stretch, model = tokens.shape
-    hidden = wup.shape[1]
+    hidden = weights[4].shape[1]
     masks = mask_positions.shape[2]
     count, half, full, width = 2 * masks, 2 * stretch, 4 * stretch, model // 2
     units = hidden // 32
     shaped = jax.ShapeDtypeStruct
     low = lambda *shape: pltpu.VMEM(shape, BF16)
     wide = lambda *shape: pltpu.VMEM(shape, F32)
-    scratch = [
+    scratch = [pltpu.VMEM(small.shape, small.dtype) for small in (segment_ids, mask_positions) + vectors]
+    scratch += [
+        wide(hidden // model + 8, model), low(width, model), low(model, model), low(model, width), low(width, full), low(width, full),
         low(full, model), low(full, model), low(model, width), low(model, width), low(model, width), low(model, model),
         low(model, hidden), low(hidden, model), low(full, width), low(full, width), low(count, width), low(count, width),
         wide(HEADS // 2, count, full), low(count, model), low(count, full), low(2, masks, width), low(2, masks, model),
@@ -887,23 +914,17 @@
         low(4 * units, 2 * model), low(4, units, 2 * model), low(2, 4, masks, model), low(2, 4, masks, model),
         wide(masks, model), wide(7, 16, model), wide(4, 16, model),
         low(full, width), low(full, width), low(half, width), wide(stretch, model), low(stretch, model), low(stretch, model),
-        low(half, model), low(half, model), wide(half, model), low(stretch, model), low(stretch, model),
+        low(stretch, model), low(stretch, model),
     ]
-    for order in ("xyz", "zyx", "xyz", "xyz"):
+    for order in ORDERS:
         size, at = model, 0
         for dim in order:
             ways = 4 if dim == "z" else 2
             size //= ways
             at += size * (ways - 1)
         scratch.append(low(at, width))
-    for order in ("xyz", "zyx", "xyz", "xyz"):
-        size, at = model, 0
-        for dim in order[:2]:
-            size //= 4 if dim == "z" else 2
-            at += size
-        scratch.append(low(at, width))
-    scratch += [pltpu.SemaphoreType.DMA((8,)), pltpu.SemaphoreType.DMA((120,)), pltpu.SemaphoreType.DMA((120,))]
-    anywhere = [pl.BlockSpec(memory_space=pl.ANY)]
+    scratch += [pltpu.SemaphoreType.DMA((8 + 2 + len(vectors),)), pltpu.SemaphoreType.DMA((120,)), pltpu.SemaphoreType.DMA((120,))]
+    anywhere = [pl.BlockSpec(memory_space=pltpu.HBM)]
     return pl.pallas_call(
         layer_kernel,
         out_shape=(
@@ -913,15 +934,16 @@
             shaped((model, model), BF16),
             shaped((model, model), BF16),
             shaped((model, model), BF16),
-            shaped((units, 2 * model), F32),
+            shaped((units, model), F32),
+            shaped((units, model), F32),
             shaped((16, model), F32),
         ),
-        in_specs=anywhere * 2 + vmem(3) + anywhere * 6,
-        out_specs=vmem(8),
+        in_specs=anywhere * (4 + len(vectors) + len(weights)),
+        out_specs=vmem(9),
         scratch_shapes=scratch,
         compiler_params=pltpu.CompilerParams(collective_id=0, has_side_effects=True, vmem_limit_bytes=62 * 2**20),
         name="layer",
-    )(tokens, cotangent, segment_ids, mask_positions, vecs, wq, wk, wv, wo, wup, wdown)
+    )(tokens, cotangent, segment_ids, mask_positions, *vectors, *weights)
 
 
 def on_device(
@@ -947,14 +969,12 @@
     second_shift,
 ):
     if rows_total == 8:
-        vecs = jnp.concatenate(
-            [up_bias]
-            + [query_bias, value_bias, output_bias, first_gain, first_shift, down_bias, second_gain, second_shift]
-        ).reshape(-1, tokens.shape[2])
-        layer_output, input_grad, go, gq, gk, gv, hidden_grads, small = layer_call(
-            tokens, cotangent, segment_ids, mask_positions, vecs, query_weight, key_weight, value_weight, output_weight, up_weight, down_weight
+        vectors = (up_bias, query_bias, value_bias, output_bias, first_gain, first_shift, down_bias, second_gain, second_shift)
+        weights = (query_weight, key_weight, value_weight, output_weight, up_weight, down_weight)
+        layer_output, input_grad, go, gq, gk, gv, up_part, down_part, small = layer_call(
+            tokens, cotangent, segment_ids, mask_positions, vectors, weights
         )
-        return outputs(layer_output, input_grad, gq, gk, gv, go, hidden_grads, small)
+        return outputs(layer_output, input_grad, gq, gk, gv, go, up_part, down_part, small)
     _, stretch, model = tokens.shape
     hidden = up_weight.shape[1]
     width = model // 2
@@ -1073,7 +1093,8 @@
         pieces.append(piece.astype(F32))
     hidden_grads = lax.psum_scatter(jnp.concatenate(pieces, axis=0), both, scatter_dimension=0, tiled=True)
 
-    return outputs(layer_output, input_grad, grad_wq, grad_wk, grad_wv, grad_wo, hidden_grads, small)
+    up_part, down_part = hidden_grads[:, :model], hidden_grads[:, model:]
+    return outputs(layer_output, input_grad, grad_wq, grad_wk, grad_wv, grad_wo, up_part, down_part, small)
 
 
 def solution(mesh):

time: 150 us -> 133 us (0.89)
  Pallas kernels: 127 us -> 117 us
  local copies, waits for them, and re-layouts: 15 us -> 7.44 us
    pallas_call x1, Pallas kernels: 127 us -> 117 us  [layer_call(): pl.pallas_call(layer_kernel, out_shape=(shaped((2, stretch, model), BF16)...]
    unnamed x22 -> x18, local copies, waits for them, and re-layouts: 8.69 us -> 4.47 us
    slice x1 -> x0, local copies, waits for them, and re-layouts: 1.9 us -> none  [outputs(): hidden_grads[:, model:]]
where the time goes in v1:
time: 133 us
  Pallas kernels  117 us (88%)
  other arithmetic  7.67 us (6%)
  local copies, waits for them, and re-layouts  7.44 us (6%)
    pallas_call x1, Pallas kernels, layer_call(): pl.pallas_call(layer_kernel, out_shape=(shaped((2, stretch, model), BF16)...  117 us
    unnamed x18, local copies, waits for them, and re-layouts  4.47 us
    convert_element_type x1, other arithmetic, outputs(): grad_wq.astype(F32)  2.94 us

profile of v1, /device:TPU:9, one launch (start us, length us, event | category | flops | bytes accessed | tf_op | source)
XLA Modules:
  0.0 132.7 jit_solution(2879328273913777792)
XLA Ops:
  0.7 116.9 %layer.1 = (bf16[2,256,768]{2,1,0:T(8,128)(2,1)}, f32[2,256,768]{2,1,0:T(8,128)}, bf16[768,768]{1,0:T(8,128)(2,1)}, bf16[768,768]{1,0:T(8,128)(2,1)}, bf16[768,7...) custom-call(bf16[2,256,768]{2,1,0:T(8,128)(2,1)} %tokens.1, ...), custom_call_target="tpu_custom_call" | custom-call | tf_op jit(solution)/shard_map/layer/pallas_call | solution.py:928
  117.6 0.7 slice.32
  118.3 1.6 %slice_reduce_fusion = (f32[768]{0:T(1024)}, f32[768]{0:T(1024)}, f32[768]{0:T(1024)}, f32[768]{0:T(1024)}, f32[768]{0:T(1024)}, /*index=5*/f32[768]{0:T(1024)}, f32[768]{0:T(1024)}, f32[768]{0:T(1024)}) fusion(f32[16,768]{1,0:T(8,128)} %get-tuple-element.29), kind=kLoop, calls=%fused_computation | loop fusion | bytes 49152 | tf_op jit(solution)/shard_map/slice | solution.py:876
  119.9 0.6 reshape.37
  120.5 0.0 copy-start.3
  120.5 2.9 %convert_element_type.12 = f32[768,768]{1,0:T(8,128)} convert(bf16[768,768]{1,0:T(8,128)(2,1)} %get-tuple-element.28) | non-fusion elementwise | flops 589824 | bytes 3538944 | tf_op jit(solution)/shard_map/convert_element_type | solution.py:880
  123.5 0.0 copy-done.3
  123.5 0.0 copy-start.2
  123.5 1.6 %convert_element_type.13 = f32[768,768]{1,0:T(8,128)} convert(bf16[768,768]{1,0:T(8,128)(2,1)S(1)} %copy-done.3) | non-fusion elementwise | flops 589824 | bytes 3538944 | tf_op jit(solution)/shard_map/convert_element_type | solution.py:882
  125.1 0.1 copy-done.2
  125.2 0.0 copy-start.1
  125.2 1.6 %convert_element_type.14 = f32[768,768]{1,0:T(8,128)} convert(bf16[768,768]{1,0:T(8,128)(2,1)S(1)} %copy-done.2) | non-fusion elementwise | flops 589824 | bytes 3538944 | tf_op jit(solution)/shard_map/convert_element_type | solution.py:883
  126.7 0.1 copy-done.1
  126.8 0.0 copy-start.4
  126.8 1.6 %convert_element_type.15 = f32[768,768]{1,0:T(8,128)} convert(bf16[768,768]{1,0:T(8,128)(2,1)S(1)} %copy-done.1) | non-fusion elementwise | flops 589824 | bytes 3538944 | tf_op jit(solution)/shard_map/convert_element_type | solution.py:885
  128.4 0.0 copy-done.4
  128.4 0.0 copy-start
  128.4 0.9 copy.40
  129.3 0.8 copy-done
  130.1 0.0 copy-start.6
  130.1 0.0 copy-start.5
  130.1 1.1 copy.41
  131.3 0.0 copy-done.6
  131.3 0.7 copy.42
  132.0 0.0 copy-done.5
  132.0 0.7 copy.43
Async XLA Ops:
  120.5 2.9 %copy-start.3 = (bf16[768,768]{1,0:T(8,128)(2,1)S(1)}, bf16[768,768]{1,0:T(8,128)(2,1)}, u32[]{:S(2)}) copy-start(bf16[768,768]{1,0:T(8,128)(2,1)} %get-tuple-element.30) | copy-start | bytes 3538948
  123.5 1.7 %copy-start.2 = (bf16[768,768]{1,0:T(8,128)(2,1)S(1)}, bf16[768,768]{1,0:T(8,128)(2,1)}, u32[]{:S(2)}) copy-start(bf16[768,768]{1,0:T(8,128)(2,1)} %get-tuple-element.31) | copy-start | bytes 3538948
  125.2 1.7 %copy-start.1 = (bf16[768,768]{1,0:T(8,128)(2,1)S(1)}, bf16[768,768]{1,0:T(8,128)(2,1)}, u32[]{:S(2)}) copy-start(bf16[768,768]{1,0:T(8,128)(2,1)} %get-tuple-element.32) | copy-start | bytes 3538948
  126.8 1.6 %copy-start.4 = (bf16[2,256,768]{2,1,0:T(8,128)(2,1)S(1)}, bf16[2,256,768]{2,1,0:T(8,128)(2,1)}, u32[]{:S(2)}) copy-start(bf16[2,256,768]{2,1,0:T(8,128)(2,1)} %get-tuple-element.60) | copy-start | bytes 2359300
  128.4 1.7 %copy-start = (f32[2,256,768]{2,1,0:T(8,128)S(1)}, f32[2,256,768]{2,1,0:T(8,128)}, u32[]{:S(2)}) copy-start(f32[2,256,768]{2,1,0:T(8,128)} %get-tuple-element.61) | copy-start | bytes 4718596
  130.1 1.1 copy-start.6
  130.1 1.9 %copy-start.5 = (f32[96,768]{1,0:T(8,128)S(1)}, f32[96,768]{1,0:T(8,128)}, u32[]{:S(2)}) copy-start(f32[96,768]{1,0:T(8,128)} %get-tuple-element.73) | copy-start | bytes 884740

commit v2 on v1

--- a/solution.py
+++ b/solution.py
@@ -14,31 +14,27 @@
 BF16 = jnp.bfloat16
 MESH = pl.DeviceIdType.MESH
 VMEM_LIMIT = 56 * 2**20
-ORDERS = ("xyz", "zxy", "xyz", "yxz")
+ORDERS = ("yxz", "yxz", "xyz", "zxy")
 PLAN = {
     "G0": ("Sr00",),
-    "G23": ("Sr30",),
-    "G1": ("Sr20", "Sr10"),
-    "dx": ("Er00", "Ss0"),
-    "a1": ("Es0", "Ss1", "Sr01"),
-    "a2": ("Ed", "Er20", "Er30", "Sr31"),
-    "a4": ("Es1", "Ss2", "Sr21"),
-    "a5": ("Er01", "Sr02", "Ef"),
-    "a6": ("Es2", "Si", "Ss3", "Er10", "Sr11", "Er31"),
-    "a7": ("Er21", "EH", "Er11", "Sr22", "Er02"),
-    "a8": ("Es3",),
-    "a9": ("Sr32",),
-    "a10": ("Er22", "Sr12"),
-    "a11": ("Ei", "Sg22"),
-    "f0": ("Er12", "Sg12", "Er32"),
-    "f1": ("Sg32",),
-    "f2": ("Eg12", "Sg11", "Eg22", "Sg21"),
-    "f3": ("Sg02",),
-    "f4": ("Eg11", "Eg32", "Sg31"),
-    "f5": ("Sg10",),
-    "f6": ("Eg02", "Sg01"),
-    "f7": ("Eg21", "Sg20", "Eg31", "Eh"),
-    "end": ("Sg30", "Eg01", "Sg00", "So", "Eg20", "St2", "Eg30", "St3", "Et2", "Eg10", "St1", "Et3", "Et1", "Eg00", "St0", "Et0", "Eo"),
+    "p0": ("Sr10",),
+    "p1": ("Sr20",),
+    "dx": ("Ss0", "Sr30"),
+    "a1": ("Es0", "Ss1", "Er20", "Sr21", "Ed", "Si", "Er00", "Sr01"),
+    "a2": ("Ef", "Er10", "Sr11"),
+    "a4": ("Es1", "Ss2"),
+    "a5": ("EH", "Es2", "Ss3", "Er11", "Sr12", "Er21", "Er01"),
+    "a6": ("Sr22",),
+    "a8": ("Er30", "Sr31"),
+    "a9": ("Ei",),
+    "f0": ("Er31", "Sr32", "Sr02"),
+    "f1": ("Er12", "Sg12"),
+    "f2": ("Es3", "Er22", "Er32", "Sg32"),
+    "f3": ("So",),
+    "f4": ("Eg32", "Sg31", "Sg22"),
+    "f5": ("Er02", "Sg02", "Eg12", "Sg11", "Eh"),
+    "f6": ("Eg31",),
+    "end": ("Sg30", "Eg11", "Sg10", "Eg22", "Sg21", "Eg02", "Sg01", "Eo", "Eg01", "Sg00", "Eg21", "Sg20", "Eg30", "St3", "Eg10", "St1", "Eg20", "St2", "Et3", "Et1", "Eg00", "St0", "Et2", "Et0"),
 }
 
 
@@ -300,12 +296,12 @@
 
 def layer_kernel(
     tokens, cotangent, segments_in, slots_in, up_bias_in, bq_in, bv_in, bo_in, g1_in, s1_in, bdown_in, g2_in, s2_in, wq, wk, wv, wo, wup, wdown,
-    layer_out, input_grad, out_o, out_q, out_k, out_v, up_out, down_out, small_out,
+    layer_out, input_grad, out_o, out_0, out_1, out_2, up_out, down_out, small_out,
     segments, slots, up_bias, bq, bv, bo, g1, s1, bdown, g2, s2, vecs, wq_t, wkv_t, wo_t, keys_t, values_t,
-    xs, cs, wq_v, wk_v, wv_v, wo_v, wup_v, wdown_v, keys, values, queries, context, probs, picked, chosen, ctx_both, gb_both,
+    xs, xs_t, cots, cot_part, cot_in, cot_sum, cot_far, dx_send, dx_in, wq_v, wk_v, wv_v, wo_v, wup_v, wdown_v, keys, values, queries, context, probs, picked, chosen, ctx_both, gb_both,
     slopes, dq_low, dkv_low, grads, hidden_grads, hidden_in, fac_normed, fac_feed, grad_h1, small_in, small_z,
     all_queries, all_context, ctx_in, total, y1_keep, out_send, igrad_send, igrad_in,
-    in_o, in_q, in_k, in_v, local_sem, send_sem, recv_sem,
+    in_o, in_0, in_1, in_2, local_sem, send_sem, recv_sem,
 ):
     z, x, y, core = place_here()
     row = y
@@ -358,7 +354,7 @@
     get_wv = local(wv.at[:, mine], wv_v, 2)
     get_small = [local(src, dst, 8 + k) for k, (src, dst) in enumerate(small_pairs)]
     get_wq = local(wq.at[:, mine], wq_v, 3)
-    own_cot = local(cotangent.at[row], cs.at[pl.ds(0, stretch)], 4)
+    own_cot = local(cotangent, cots, 4)
     get_wo = local(wo, wo_v, 5)
     get_up = local(wup, wup_v, 6)
     get_down = local(wdown, wdown_v, 7)
@@ -375,7 +371,6 @@
         push(tokens.at[1 - row, pl.ds(k * piece, piece)], xs.at[pl.ds(stretch + k * piece, piece)], k, at_y) for k in range(2)
     ]
     tok_c = push(tokens.at[row], xs.at[pl.ds(half, stretch)], 2, twin)
-    cot_c = push(cotangent.at[row], cs.at[pl.ds(half, stretch)], 4, twin)
 
     for copy in get_small:
         copy.wait()
@@ -391,6 +386,7 @@
         block_values = (dot(block, wv_v[...]) + half_vector(5)).astype(BF16)
         keys[here, :] = block_keys
         values[here, :] = block_values
+        xs_t[:, here] = block.T
         keys_t[:, here] = block_keys.T
         values_t[:, here] = block_values.T
 
@@ -401,11 +397,22 @@
     split = jnp.sum((1 - seg_here).astype(F32), axis=1, keepdims=True)
     pos_row = pos_row.astype(F32)
     seg_row = jnp.where(pos_row >= split, 1.0, 0.0)
-    slot_rows = slots[row].astype(F32)
     diagonal = lax.broadcasted_iota(jnp.int32, (masks, masks), 0) == lax.broadcasted_iota(jnp.int32, (masks, masks), 1)
+
+    def slot_column(which, sequence):
+        line = slots[which].astype(F32)[sequence : sequence + 1, :]
+        return jnp.sum(jnp.where(diagonal, line, 0.0), axis=1, keepdims=True)
+
     for sequence in range(2):
-        column = jnp.sum(jnp.where(diagonal, slot_rows[sequence : sequence + 1, :], 0.0), axis=1, keepdims=True)
+        column = slot_column(row, sequence)
         chosen[sequence * masks : (sequence + 1) * masks, :] = jnp.where(column == pos_row, 1.0, 0.0).astype(BF16)
+    own_cot.wait()
+    for sequence in range(2):
+        here = chosen[sequence * masks : (sequence + 1) * masks, :stretch]
+        cot_part[0, sequence] = dot(here, cots[row]).astype(BF16)
+        there = jnp.where(slot_column(1 - row, sequence) == pos_row[:, :stretch], 1.0, 0.0).astype(BF16)
+        cot_part[1, sequence] = dot(there, cots[1 - row]).astype(BF16)
+    cot_c = push(cot_part.at[:, 1 - core], cot_in, 4, twin)
 
     own_tokens.wait()
     get_wk.wait()
@@ -414,15 +421,19 @@
     tok_c.wait_recv()
     key_values(half)
     get_wq.wait()
-    wkv_t[:width, :] = wk_v[...].T
-    wkv_t[width:, :] = wv_v[...].T
+    for pair in range(width // 128):
+        lanes = slice(pair * 128, pair * 128 + 128)
+        wkv_t[pair * 256 : pair * 256 + 128, :] = wk_v[:, lanes].T
+        wkv_t[pair * 256 + 128 : pair * 256 + 256, :] = wv_v[:, lanes].T
     wq_t[...] = wq_v[...].T
     forward = []
     for k in range(2):
         tok_y[k].wait_recv()
         src = xs.at[pl.ds(stretch + k * piece, piece)]
         forward.append(push(src, xs.at[pl.ds(half + stretch + k * piece, piece)], 5 + k, twin))
-    cot_y = push(cotangent.at[1 - row], cs.at[pl.ds(stretch, stretch)], 3, at_y)
+    cot_c.wait_recv()
+    cot_sum[...] = cot_part[:, core] + cot_in[...]
+    cot_y = push(cot_sum.at[1], cot_far, 3, at_y)
     key_values(stretch)
     for copy in forward:
         copy.wait_recv()
@@ -445,16 +456,14 @@
             scores = jnp.where(same, dot(head_queries, pair_keys), MASKED_SCORE)
             weights = jnp.exp(scores - jnp.max(scores, axis=-1, keepdims=True))
             share = weights / jnp.sum(weights, axis=-1, keepdims=True)
+            share = share.astype(BF16)
             probs[pair * 2 + side] = share
-            outs.append(dot(share.astype(BF16), pair_values))
+            outs.append(dot(share, pair_values))
         first = lane_is((count, 128), 0, 64)
         context[:, lanes] = jnp.where(first, outs[0], outs[1]).astype(BF16)
     ctx_both[core] = context[my_slots, :]
     ctx_c = push(context.at[twin_slots], ctx_both.at[core], 7, twin)
 
-    own_cot.wait()
-    cot_y.wait_recv()
-    cot_f = push(cs.at[pl.ds(stretch, stretch)], cs.at[pl.ds(half + stretch, stretch)], 8, twin)
     for start in range(0, full, stretch):
         value = (dot(xs[start : start + stretch, :], wq_v[...]) + half_vector(4)).astype(BF16)
         all_queries[start : start + stretch, :] = (value.astype(F32) * 0.125).astype(BF16)
@@ -478,9 +487,8 @@
         slopes[part] = slope
         sum2 = sum2 + dot(act.astype(BF16), wdown_v[there, :])
     n2, r2 = norm_parts(sum2)
-    cot_c.wait_recv()
-    cot_f.wait_recv()
-    grad = dot(chosen[my_slots, :], cs[...])
+    cot_y.wait_recv()
+    grad = cot_sum[0].astype(F32) + cot_far[...].astype(F32)
     gh2 = norm_back(grad, n2, r2, vector(10))
     gf = gh2.astype(BF16)
     fac_feed[core, z] = gf
@@ -508,8 +516,8 @@
     sizes = {"x": 2, "y": 2, "z": 4}
     dims = {"x": [at_x], "y": [at_y], "z": columns}
     orders = ORDERS
-    ins = [in_o, in_q, in_k, in_v]
-    outs = [out_o, out_q, out_k, out_v]
+    ins = [in_o, in_0, in_1, in_2]
+    outs = [out_o, out_0, out_1, out_2]
 
     def regions(job):
         base, size, found = 0, model, [(0, model)]
@@ -527,11 +535,6 @@
         return at, size // sizes[orders[job][stage]]
 
     def out_at(job, base, size):
-        if job == 0:
-            side = base // width
-            offset = base - side * width
-            at = pl.ds(pl.multiple_of(core * width + offset, 16), size)
-            return outs[0].at[at, pl.ds(pl.multiple_of(side * width, 128), width)]
         return outs[job].at[pl.ds(pl.multiple_of(base, 16), size), mine]
 
     def reduce_copies(job, stage):
@@ -575,7 +578,7 @@
         ]
 
     def twin_copy(job):
-        spot = outs[0].at[mine, :] if job == 0 else outs[job].at[:, mine]
+        spot = outs[job].at[:, mine]
         return remote(spot, spot, 40 + job * 20 + 18, twin)
 
     def gather_start(job, stage):
@@ -674,9 +677,9 @@
         return remote(igrad_send, igrad_in, 29, at_y)
 
     def igrad_step():
-        remote(cs.at[pl.ds(0, half)], cs.at[pl.ds(half, half)], 28, twin).wait_recv()
-        input_grad[row] = input_grad[row] + cs[half : half + stretch, :].astype(F32)
-        igrad_send[...] = (input_grad[1 - row] + cs[half + stretch :, :].astype(F32)).astype(BF16)
+        remote(dx_send, dx_in, 28, twin).wait_recv()
+        input_grad[row] = input_grad[row] + dx_in[:stretch, :].astype(F32)
+        igrad_send[...] = (input_grad[1 - row] + dx_in[stretch:, :].astype(F32)).astype(BF16)
 
     def igrad_end():
         igrad_copy().wait()
@@ -714,9 +717,7 @@
 
     gb = gb_both[...].reshape(count, model)
     gctx = dot(gb, wo_t[...]).astype(BF16)
-    value = dot_tn(context[...], gb).astype(BF16)
-    grads[0, :width, :] = value[:, :width]
-    grads[0, width:, :] = value[:, width:]
+    grads[0] = dot_tn(gb, context[...]).astype(BF16)
     act_on("G0")
     for pair in range(pairs):
         lanes = slice(pair * 128, pair * 128 + 128)
@@ -726,28 +727,29 @@
         for side in range(2):
             keep = lane_is((count, 128), side * 64, side * 64 + 64)
             head_gctx = jnp.where(keep, pair_gctx.astype(F32), 0.0).astype(BF16)
-            share = probs[pair * 2 + side]
+            low_share = probs[pair * 2 + side]
+            share = low_share.astype(F32)
             gp = dot(head_gctx, pair_values)
             spread = jnp.sum(share * gp, axis=-1, keepdims=True)
             gs = (share * (gp - spread)).astype(BF16)
             dqs.append(dot(gs, pair_keys))
             dks.append(dot_tn(gs, pair_queries))
-            dvs.append(dot_tn(share.astype(BF16), pair_gctx))
+            dvs.append(dot_tn(low_share, pair_gctx))
         first = lane_is((count, 128), 0, 64)
-        dq_low[:, lanes] = (jnp.where(first, dqs[0], dqs[1]) * 0.125).astype(BF16)
+        dq = (jnp.where(first, dqs[0], dqs[1]) * 0.125).astype(BF16)
+        dq_low[:, lanes] = dq
         first = lane_is((full, 128), 0, 64)
-        dkv_low[:, lanes] = (jnp.where(first, dks[0], dks[1]) * 0.125).astype(BF16)
-        dkv_low[:, width + pair * 128 : width + pair * 128 + 128] = jnp.where(first, dvs[0], dvs[1]).astype(BF16)
-    act_on("heads")
-    for start in range(0, model, 256):
-        value = dot_tn(xs[:, start : start + 256], dkv_low[...]).astype(BF16)
-        grads[2, start : start + 256, :] = value[:, :width]
-        grads[3, start : start + 256, :] = value[:, width:]
-    act_on("G23")
-    grads[1] = dot_tn(picked[...], dq_low[...]).astype(BF16)
-    act_on("G1")
-    small_in[0, parts + 6 : parts + 7, mine] = jnp.sum(dq_low[...].astype(F32), axis=0, keepdims=True)
-    small_in[0, parts + 7 : parts + 8, mine] = jnp.sum(dkv_low[:, width:].astype(F32), axis=0, keepdims=True)
+        dk = (jnp.where(first, dks[0], dks[1]) * 0.125).astype(BF16)
+        dv = jnp.where(first, dvs[0], dvs[1]).astype(BF16)
+        both = slice(pair * 256, pair * 256 + 256)
+        dkv_low[:, pair * 256 : pair * 256 + 128] = dk
+        dkv_low[:, pair * 256 + 128 : pair * 256 + 256] = dv
+        grads[1 + pair, :, :128] = dot_tn(picked[...], dq).astype(BF16)
+        grads[1 + pair, :, 128:] = dot(xs_t[...], dkv_low[:, both]).astype(BF16)
+        act_on("p" + str(pair))
+        there = pl.ds(pl.multiple_of(core * width + pair * 128, 128), 128)
+        small_in[0, parts + 6 : parts + 7, there] = jnp.sum(dq.astype(F32), axis=0, keepdims=True)
+        small_in[0, parts + 7 : parts + 8, there] = jnp.sum(dv.astype(F32), axis=0, keepdims=True)
 
     spread_rows = dot(dq_low[...], wq_t[...])
     zero = jnp.zeros((masks, model), F32)
@@ -756,8 +758,6 @@
     spread_rows = spread_rows + jnp.concatenate([jnp.where(is_first, gh1, zero), jnp.where(is_first, zero, gh1)], axis=0)
     high = spread_rows.astype(BF16)
     rest = (spread_rows - high.astype(F32)).astype(BF16)
-    cot_f.wait_send()
-    pending[:] = [copy for copy in pending if copy is not cot_f]
     for start in (half, half + stretch, 0, stretch):
         here = slice(start, start + stretch)
         value = dot_tn(chosen[:, here], high) + dot_tn(chosen[:, here], rest)
@@ -765,9 +765,9 @@
         if start < half:
             input_grad[row if start == 0 else 1 - row] = value
         else:
-            cs[start - half : start - half + stretch, :] = value.astype(BF16)
+            dx_send[start - half : start - half + stretch, :] = value.astype(BF16)
             if start > half:
-                push(cs.at[pl.ds(0, half)], cs.at[pl.ds(half, half)], 28, twin)
+                push(dx_send, dx_in, 28, twin)
 
     act_on("dx")
 
@@ -868,6 +868,54 @@
         )(core, *operands)
 
     return call
+
+
+def finish_kernel(parts, go, g0, g1, g2, layer_in, igrad_in, up_in, down_in, small, wq, wk, wv, wo, layer_out, igrad, up, down, up_bias, *vectors):
+    wo[...] = go[...].T.astype(F32)
+    for pair, ref in enumerate((g0, g1, g2)):
+        for core in range(2):
+            at = core * 384 + pair * 128
+            for place, out in enumerate((wq, wk, wv)):
+                begin = core * 384 + place * 128
+                out[:, at : at + 128] = ref[:, begin : begin + 128].astype(F32)
+    layer_out[...] = layer_in[...]
+    igrad[...] = igrad_in[...]
+    up[...] = up_in[...]
+    down[...] = down_in[...]
+
+    @pl.when(pl.program_id(0) == 0)
+    def _():
+        model = small.shape[1]
+        for part in range(parts):
+            up_bias[part * model : (part + 1) * model] = small[part]
+        for place, out in enumerate(vectors):
+            out[...] = small[parts + place]
+
+
+def finish(layer_output, input_grad, go, g0, g1, g2, up_part, down_part, small, hidden):
+    model = go.shape[0]
+    stretch, units, parts = layer_output.shape[1], up_part.shape[0], hidden // model
+    shaped = jax.ShapeDtypeStruct
+    rows = pl.BlockSpec((128, model), lambda i: (i, 0))
+    columns = pl.BlockSpec((model, 128), lambda i: (0, i))
+    tokens = pl.BlockSpec((2, stretch, 128), lambda i: (0, 0, i))
+    unit = pl.BlockSpec((units, 128), lambda i: (0, i))
+    line = pl.BlockSpec((model,), lambda i: (0,))
+    square, vector = shaped((model, model), F32), shaped((model,), F32)
+    found = pl.pallas_call(
+        functools.partial(finish_kernel, parts),
+        grid=(model // 128,),
+        out_shape=(square,) * 4
+        + (shaped(layer_output.shape, BF16), shaped(input_grad.shape, F32), shaped(up_part.shape, F32), shaped(down_part.shape, F32))
+        + (shaped((hidden,), F32),)
+        + (vector,) * 8,
+        in_specs=[columns, rows, rows, rows, tokens, tokens, unit, unit, pl.BlockSpec(small.shape, lambda i: (0, 0))],
+        out_specs=[rows] * 4 + [tokens, tokens, unit, unit, pl.BlockSpec((hidden,), lambda i: (0,))] + [line] * 8,
+        compiler_params=pltpu.CompilerParams(vmem_limit_bytes=VMEM_LIMIT),
+        name="finish",
+    )(go, g0, g1, g2, layer_output, input_grad, up_part, down_part, small)
+    wq, wk, wv, wo, layer_output, input_grad, up_part, down_part, up_bias, g1, s1, g2, s2, ob, db, qb, vb = found
+    return layer_output, input_grad, wq, qb, wk, wv, vb, wo, ob, g1, s1, up_part.T, up_bias, down_part, db, g2, s2
 
 
 def outputs(layer_output, input_grad, grad_wq, grad_wk, grad_wv, grad_wo, up_part, down_part, small):
@@ -907,9 +955,10 @@
     scratch = [pltpu.VMEM(small.shape, small.dtype) for small in (segment_ids, mask_positions) + vectors]
     scratch += [
         wide(hidden // model + 8, model), low(width, model), low(model, model), low(model, width), low(width, full), low(width, full),
-        low(full, model), low(full, model), low(model, width), low(model, width), low(model, width), low(model, model),
+        low(full, model), low(model, full), low(2, stretch, model), low(2, 2, masks, model), low(2, masks, model), low(2, masks, model),
+        low(masks, model), low(half, model), low(half, model), low(model, width), low(model, width), low(model, width), low(model, model),
         low(model, hidden), low(hidden, model), low(full, width), low(full, width), low(count, width), low(count, width),
-        wide(HEADS // 2, count, full), low(count, model), low(count, full), low(2, masks, width), low(2, masks, model),
+        low(HEADS // 2, count, full), low(count, model), low(count, full), low(2, masks, width), low(2, masks, model),
         wide(hidden // model, masks, model), low(count, width), low(full, model), low(4, model, width),
         low(4 * units, 2 * model), low(4, units, 2 * model), low(2, 4, masks, model), low(2, 4, masks, model),
         wide(masks, model), wide(7, 16, model), wide(4, 16, model),
@@ -971,10 +1020,10 @@
     if rows_total == 8:
         vectors = (up_bias, query_bias, value_bias, output_bias, first_gain, first_shift, down_bias, second_gain, second_shift)
         weights = (query_weight, key_weight, value_weight, output_weight, up_weight, down_weight)
-        layer_output, input_grad, go, gq, gk, gv, up_part, down_part, small = layer_call(
+        found = layer_call(
             tokens, cotangent, segment_ids, mask_positions, vectors, weights
         )
-        return outputs(layer_output, input_grad, gq, gk, gv, go, up_part, down_part, small)
+        return finish(*found, up_weight.shape[1])
     _, stretch, model = tokens.shape
     hidden = up_weight.shape[1]
     width = model // 2

time: 133 us -> 122 us (0.917)
  other arithmetic: 7.67 us -> 0 us
  local copies, waits for them, and re-layouts: 7.44 us -> 0 us
  Pallas kernels: 117 us -> 121 us
    pallas_call x0 -> x1, Pallas kernels: none -> 9.08 us  [finish(): pl.pallas_call(functools.partial(finish_kernel, parts), grid=(model // 12...]
    convert_element_type x4 -> x0, other arithmetic: 7.67 us -> none  [the longest x1 2.94 us: outputs(): grad_wq.astype(F32)]
    pallas_call x1, Pallas kernels: 117 us -> 112 us  [layer_call(): pl.pallas_call(layer_kernel, out_shape=(shaped((2, stretch, model), BF16)...]
    unnamed x18 -> x0, local copies, waits for them, and re-layouts: 4.47 us -> none
    slice x2 -> x0, local copies, waits for them, and re-layouts: 2.37 us -> none  [the longest x1 1.63 us: outputs(): vector = lambda index: small[index]]
where the time goes in v2:
time: 122 us
  Pallas kernels  121 us (99%)
    pallas_call x1, Pallas kernels, layer_call(): pl.pallas_call(layer_kernel, out_shape=(shaped((2, stretch, model), BF16)...  112 us
    pallas_call x1, Pallas kernels, finish(): pl.pallas_call(functools.partial(finish_kernel, parts), grid=(model // 12...  9.08 us

profile of v2, /device:TPU:9, one launch (start us, length us, event | category | flops | bytes accessed | tf_op | source)
XLA Modules:
  0.0 122.0 jit_solution(12371384376953045952)
XLA Ops:
  0.7 112.0 %layer.1 = (bf16[2,256,768]{2,1,0:T(8,128)(2,1)}, f32[2,256,768]{2,1,0:T(8,128)}, bf16[768,768]{1,0:T(8,128)(2,1)}, bf16[768,768]{1,0:T(8,128)(2,1)}, bf16[768,7...) custom-call(bf16[2,256,768]{2,1,0:T(8,128)(2,1)} %tokens.1, ...), custom_call_target="tpu_custom_call" | custom-call | tf_op jit(solution)/shard_map/layer/pallas_call | solution.py:977
  112.7 9.1 %finish.1 = (f32[768,768]{1,0:T(8,128)}, f32[768,768]{1,0:T(8,128)}, f32[768,768]{1,0:T(8,128)}, f32[768,768]{1,0:T(8,128)}, bf16[2,256,768]{2,1,0:T(8,128)(2,1)...) custom-call(bf16[768,768]{1,0:T(8,128)(2,1)} %get-tuple-element.43.g, ...), custom_call_target="tpu_custom_call" | custom-call | tf_op jit(solution)/shard_map/finish/pallas_call | solution.py:905

commit v3 on v2

--- a/solution.py
+++ b/solution.py
@@ -14,27 +14,26 @@
 BF16 = jnp.bfloat16
 MESH = pl.DeviceIdType.MESH
 VMEM_LIMIT = 56 * 2**20
-ORDERS = ("yxz", "yxz", "xyz", "zxy")
+ORDERS = ("xyz", "yxz", "xyz", "xyz")
 PLAN = {
-    "G0": ("Sr00",),
-    "p0": ("Sr10",),
-    "p1": ("Sr20",),
-    "dx": ("Ss0", "Sr30"),
-    "a1": ("Es0", "Ss1", "Er20", "Sr21", "Ed", "Si", "Er00", "Sr01"),
-    "a2": ("Ef", "Er10", "Sr11"),
-    "a4": ("Es1", "Ss2"),
-    "a5": ("EH", "Es2", "Ss3", "Er11", "Sr12", "Er21", "Er01"),
-    "a6": ("Sr22",),
-    "a8": ("Er30", "Sr31"),
-    "a9": ("Ei",),
-    "f0": ("Er31", "Sr32", "Sr02"),
-    "f1": ("Er12", "Sg12"),
-    "f2": ("Es3", "Er22", "Er32", "Sg32"),
-    "f3": ("So",),
-    "f4": ("Eg32", "Sg31", "Sg22"),
-    "f5": ("Er02", "Sg02", "Eg12", "Sg11", "Eh"),
-    "f6": ("Eg31",),
-    "end": ("Sg30", "Eg11", "Sg10", "Eg22", "Sg21", "Eg02", "Sg01", "Eo", "Eg01", "Sg00", "Eg21", "Sg20", "Eg30", "St3", "Eg10", "St1", "Eg20", "St2", "Et3", "Et1", "Eg00", "St0", "Et2", "Et0"),
+    "G0": ("Sr00", "Sr01"),
+    "p0": ("Sr10", "Sr11"),
+    "p1": ("Sr20", "Sr21"),
+    "p2": ("Sr30", "Sr31", "Er00", "Sr02"),
+    "dx": ("Ss0", "Er10", "Sr12", "Er01", "Er11", "Er20", "Sr22"),
+    "a1": ("Ed", "Si0", "Ef", "Es0", "Ss1", "Er21", "Er02", "Sr03"),
+    "a2": ("Er22", "Sr23", "Er30", "Sr32", "EH", "Si1", "Sh0", "Es1", "Ss2", "Ei0", "Er12", "Sr13", "Er03", "Sg03", "Er31", "Er23", "Sg23", "Er32", "Sr33"),
+    "a4": ("Sh1",),
+    "a5": ("Er13", "Sg13", "Ei1"),
+    "a6": ("Es2", "Ss3", "Eg03", "Sg00", "Sg02"),
+    "a9": ("Eg23", "Sg20", "Sg22"),
+    "a11": ("Er33", "Sg33"),
+    "f0": ("Eg00",),
+    "f1": ("Eg13", "Sg10", "Sg12", "Eh"),
+    "f2": ("Es3", "Eg20", "Eg02", "St00", "Sg01"),
+    "f4": ("So0", "Eg22", "St20", "Sg21", "Eg33", "Sg30", "Sg32", "Et00", "Eg12", "St10", "Sg11"),
+    "f6": ("Et20", "Eg10", "Eg01", "St01", "Et10"),
+    "end": ("Eg21", "St21", "Et01", "Eo0", "So1", "Et21", "Eg30", "Eg32", "St30", "Sg31", "Et30", "Eg11", "St11", "Eg31", "St31", "Et11", "Eo1", "Et31"),
 }
 
 
@@ -296,6 +295,7 @@
 
 def layer_kernel(
     tokens, cotangent, segments_in, slots_in, up_bias_in, bq_in, bv_in, bo_in, g1_in, s1_in, bdown_in, g2_in, s2_in, wq, wk, wv, wo, wup, wdown,
+    layer_hbm, igrad_hbm, hbm_o, hbm_0, hbm_1, hbm_2, up_hbm, down_hbm, small_hbm,
     layer_out, input_grad, out_o, out_0, out_1, out_2, up_out, down_out, small_out,
     segments, slots, up_bias, bq, bv, bo, g1, s1, bdown, g2, s2, vecs, wq_t, wkv_t, wo_t, keys_t, values_t,
     xs, xs_t, cots, cot_part, cot_in, cot_sum, cot_far, dx_send, dx_in, wq_v, wk_v, wv_v, wo_v, wup_v, wdown_v, keys, values, queries, context, probs, picked, chosen, ctx_both, gb_both,
@@ -512,82 +512,76 @@
         small_in[0, parts + place : parts + place + 1, :] = jnp.sum(value, axis=0, keepdims=True)
     gb_c.wait_recv()
 
-    spots = {"x": x, "y": y, "z": z}
-    sizes = {"x": 2, "y": 2, "z": 4}
-    dims = {"x": [at_x], "y": [at_y], "z": columns}
-    orders = ORDERS
+    spots = {"x": x, "y": y}
+    neighbours = {"x": at_x, "y": at_y}
     ins = [in_o, in_0, in_1, in_2]
     outs = [out_o, out_0, out_1, out_2]
-
-    def regions(job):
-        base, size, found = 0, model, [(0, model)]
-        for dim in orders[job]:
-            size = size // sizes[dim]
-            base = base + spots[dim] * size
-            found.append((base, size))
-        return found
-
-    def in_place(job, stage):
-        at, size = 0, model
-        for dim in orders[job][:stage]:
-            size = size // sizes[dim]
-            at += size * (sizes[dim] - 1)
-        return at, size // sizes[orders[job][stage]]
-
-    def out_at(job, base, size):
-        return outs[job].at[pl.ds(pl.multiple_of(base, 16), size), mine]
-
-    def reduce_copies(job, stage):
-        dim = orders[job][stage]
-        at, size = in_place(job, stage)
-        base, _ = regions(job)[stage]
-        copies = []
-        for k, target in enumerate(dims[dim]):
-            other = (spots[dim] + k + 1) % sizes[dim]
-            src = grads.at[job, pl.ds(pl.multiple_of(base + other * size, 16), size)]
-            dst = ins[job].at[pl.ds(at + k * size, size)]
-            copies.append(remote(src, dst, 40 + job * 20 + stage * 3 + k, target))
-        return copies
-
-    def reduce_start(job, stage):
-        for copy in reduce_copies(job, stage):
+    half_rows, quarter, chunk = model // 2, model // 4, model // 16
+
+    def rows_of(job):
+        p1, p2 = (spots[dim] for dim in ORDERS[job][:2])
+        kept, gone = p1 * half_rows, (1 - p1) * half_rows
+        return kept, kept + p2 * quarter, kept + (1 - p2) * quarter, kept + p2 * quarter + z * chunk, gone + (1 - p2) * quarter, gone + p2 * quarter
+
+    def at(start, size):
+        return pl.ds(pl.multiple_of(start, 16), size)
+
+    def job_copies(kind, job, stage):
+        first, second = (neighbours[dim] for dim in ORDERS[job][:2])
+        kept, mine_at, pass_at, own, gone_pass, gone_keep = rows_of(job)
+        source, arrive, out = grads.at[job], ins[job], outs[job]
+        base = 40 + job * 16
+
+        def spread(start, size, index, target):
+            spot = out.at[at(start, size), mine]
+            return remote(spot, spot, base + index, target)
+
+        if kind == "r" and stage == 0:
+            return [remote(source.at[at(gone_pass, quarter)], arrive.at[pl.ds(0, quarter)], base, first)]
+        if kind == "r" and stage == 1:
+            return [remote(source.at[at(gone_keep, quarter)], arrive.at[pl.ds(quarter, quarter)], base + 1, first)]
+        if kind == "r" and stage == 2:
+            return [remote(source.at[at(pass_at, quarter)], arrive.at[pl.ds(2 * quarter, quarter)], base + 2, second)]
+        if kind == "r":
+            return [
+                remote(
+                    source.at[at(mine_at + others[k] * chunk, chunk)], arrive.at[pl.ds(3 * quarter + k * chunk, chunk)], base + 3 + k, columns[k]
+                )
+                for k in range(3)
+            ]
+        if kind == "g" and stage == 3:
+            return [spread(own, chunk, 6 + k, columns[k]) for k in range(3)]
+        if kind == "g" and stage == 2:
+            return [spread(mine_at, quarter, 9, second)]
+        if kind == "g" and stage == 0:
+            return [spread(mine_at, quarter, 10, first)]
+        if kind == "g":
+            return [spread(pass_at, quarter, 11, first)]
+        return [spread(kept if stage == 0 else half_rows - kept, half_rows, 12 + stage, twin)]
+
+    def job_start(kind, job, stage):
+        for copy in job_copies(kind, job, stage):
             copy.start()
 
-    def reduce_end(job, stage):
-        for copy in reduce_copies(job, stage):
+    def job_end(kind, job, stage):
+        for copy in job_copies(kind, job, stage):
             copy.wait()
-        dim = orders[job][stage]
-        at, size = in_place(job, stage)
-        base, _ = regions(job)[stage + 1]
-        here = pl.ds(pl.multiple_of(base, 16), size)
-        value = grads[job, here].astype(F32)
-        for k in range(len(dims[dim])):
-            value = value + ins[job][pl.ds(at + k * size, size)].astype(F32)
-        value = value.astype(BF16)
-        if stage < 2:
-            grads[job, here] = value
-        else:
-            out_at(job, base, size)[...] = value
-
-    def gather_copies(job, stage):
-        base, size = regions(job)[stage + 1]
-        spot = out_at(job, base, size)
-        return [
-            remote(spot, spot, 40 + job * 20 + 9 + stage * 3 + k, target)
-            for k, target in enumerate(dims[orders[job][stage]])
-        ]
-
-    def twin_copy(job):
-        spot = outs[job].at[:, mine]
-        return remote(spot, spot, 40 + job * 20 + 18, twin)
-
-    def gather_start(job, stage):
-        for copy in gather_copies(job, stage):
-            copy.start()
-
-    def gather_end(job, stage):
-        for copy in gather_copies(job, stage):
-            copy.wait()
+        if kind != "r":
+            return
+        _, mine_at, pass_at, own, _, _ = rows_of(job)
+        arrive = ins[job]
+        if stage == 0:
+            here = at(pass_at, quarter)
+            grads[job, here] = (grads[job, here].astype(F32) + arrive[:quarter].astype(F32)).astype(BF16)
+        elif stage == 2:
+            here = at(mine_at, quarter)
+            value = grads[job, here].astype(F32) + arrive[quarter : 2 * quarter].astype(F32)
+            grads[job, here] = (value + arrive[2 * quarter : 3 * quarter].astype(F32)).astype(BF16)
+        elif stage == 3:
+            value = grads[job, at(own, chunk)].astype(F32)
+            for k in range(3):
+                value = value + arrive[3 * quarter + k * chunk : 3 * quarter + (k + 1) * chunk].astype(F32)
+            outs[job][at(own, chunk), mine] = value.astype(BF16)
 
     def small_copies(stage):
         if stage < 3:
@@ -644,13 +638,15 @@
         hidden_grads[:, model:] = dot_tn(act.astype(BF16), feed).astype(BF16)
         for cy in range(2):
             for cc in range(2):
-                @pl.when(jnp.logical_not(is_me(cy, cc)))
-                def _(cy=cy, cc=cc):
-                    hidden_copy(cy, cc).start()
-
                 @pl.when(is_me(cy, cc))
                 def _(cy=cy, cc=cc):
                     hidden_in[source] = hidden_grads[pl.ds((cy * 2 + cc) * units, units)]
+
+    def hidden_start(cc):
+        for cy in range(2):
+            @pl.when(jnp.logical_not(is_me(cy, cc)))
+            def _(cy=cy):
+                hidden_copy(cy, cc).start()
 
     def hidden_end():
         for cy in range(2):
@@ -673,43 +669,72 @@
         up_out[...] = value[:, :model]
         down_out[...] = value[:, model:]
 
-    def igrad_copy():
-        return remote(igrad_send, igrad_in, 29, at_y)
+    def piece_of(index):
+        return pl.ds(index * piece, piece)
+
+    def igrad_copy(index):
+        return remote(igrad_send.at[piece_of(index)], igrad_in.at[piece_of(index)], 29 + index, at_y)
 
     def igrad_step():
         remote(dx_send, dx_in, 28, twin).wait_recv()
         input_grad[row] = input_grad[row] + dx_in[:stretch, :].astype(F32)
         igrad_send[...] = (input_grad[1 - row] + dx_in[stretch:, :].astype(F32)).astype(BF16)
 
-    def igrad_end():
-        igrad_copy().wait()
-        input_grad[1 - row] = igrad_in[...].astype(F32)
-
-    def out_copy():
-        return remote(out_send, layer_out.at[row], 31, at_y)
+    def igrad_end(index):
+        igrad_copy(index).wait()
+        input_grad[1 - row, piece_of(index)] = igrad_in[piece_of(index), :].astype(F32)
+
+    def out_copy(index):
+        return remote(out_send.at[piece_of(index)], layer_out.at[row, piece_of(index)], 32 + index, at_y)
+
+    results = [
+        (layer_out, layer_hbm), (input_grad, igrad_hbm), (out_o, hbm_o), (out_0, hbm_0), (out_1, hbm_1), (out_2, hbm_2),
+        (up_out, up_hbm), (down_out, down_hbm), (small_out, small_hbm),
+    ]
+
+    def result_copy(index):
+        src, dst = results[index]
+        return pltpu.make_async_copy(src, dst, local_sem.at[20 + index])
+
+    ended = []
 
     def act(name):
         start, kind, rest = name[0] == "S", name[1], [int(c) for c in name[2:]]
-        if kind == "r":
-            (reduce_start if start else reduce_end)(*rest)
-        elif kind == "g":
-            (gather_start if start else gather_end)(*rest)
-        elif kind == "t":
-            twin_copy(*rest).start() if start else twin_copy(*rest).wait()
+        ended.append(name)
+        if kind in "rgt":
+            (job_start if start else job_end)(kind, *rest)
+            if kind == "t" and not start and {"Et%d0" % rest[0], "Et%d1" % rest[0]} <= set(ended):
+                result_copy(2 + rest[0]).start()
         elif kind == "s":
             (small_start if start else small_end)(*rest)
+            if not start and rest[0] == 3:
+                result_copy(8).start()
         elif kind == "d":
             igrad_step()
         elif kind == "i":
-            igrad_copy().start() if start else igrad_end()
+            if start:
+                igrad_copy(*rest).start()
+            else:
+                igrad_end(*rest)
+                if {"Ei0", "Ei1"} <= set(ended):
+                    result_copy(1).start()
         elif kind == "o":
-            out_copy().start() if start else out_copy().wait()
+            if start:
+                out_copy(*rest).start()
+            else:
+                out_copy(*rest).wait()
+                if {"Eo0", "Eo1"} <= set(ended):
+                    result_copy(0).start()
         elif kind == "f":
             factors_on()
         elif kind == "H":
             hidden_make()
+        elif kind == "h" and start:
+            hidden_start(*rest)
         elif kind == "h":
             hidden_end()
+            result_copy(6).start()
+            result_copy(7).start()
 
     def act_on(name):
         for each in PLAN.get(name, ()):
@@ -779,7 +804,7 @@
                     act_on(prefix + str(at))
 
     def ctx_copy():
-        return remote(all_context.at[pl.ds(half, half)], ctx_in, 30, twin)
+        return remote(all_context.at[pl.ds(half, half)], ctx_in, 31, twin)
 
     def attend_step(step, carry):
         tile, pair = (step // pairs + 2) % 4, step % pairs
@@ -847,6 +872,8 @@
 
     lax.fori_loop(0, 2 * parts, feed_step, 0)
     act_on("end")
+    for index in range(len(results)):
+        result_copy(index).wait()
     for copy in pending:
         copy.wait_send()
 
@@ -952,7 +979,9 @@
     shaped = jax.ShapeDtypeStruct
     low = lambda *shape: pltpu.VMEM(shape, BF16)
     wide = lambda *shape: pltpu.VMEM(shape, F32)
-    scratch = [pltpu.VMEM(small.shape, small.dtype) for small in (segment_ids, mask_positions) + vectors]
+    results = [low(2, stretch, model), wide(2, stretch, model)] + [low(model, model)] * 4
+    results += [wide(units, model), wide(units, model), wide(16, model)]
+    scratch = results + [pltpu.VMEM(small.shape, small.dtype) for small in (segment_ids, mask_positions) + vectors]
     scratch += [
         wide(hidden // model + 8, model), low(width, model), low(model, model), low(model, width), low(width, full), low(width, full),
         low(full, model), low(model, full), low(2, stretch, model), low(2, 2, masks, model), low(2, masks, model), low(2, masks, model),
@@ -965,14 +994,8 @@
         low(full, width), low(full, width), low(half, width), wide(stretch, model), low(stretch, model), low(stretch, model),
         low(stretch, model), low(stretch, model),
     ]
-    for order in ORDERS:
-        size, at = model, 0
-        for dim in order:
-            ways = 4 if dim == "z" else 2
-            size //= ways
-            at += size * (ways - 1)
-        scratch.append(low(at, width))
-    scratch += [pltpu.SemaphoreType.DMA((8 + 2 + len(vectors),)), pltpu.SemaphoreType.DMA((120,)), pltpu.SemaphoreType.DMA((120,))]
+    scratch += [low(model - model // 16, width)] * 4
+    scratch += [pltpu.SemaphoreType.DMA((32,)), pltpu.SemaphoreType.DMA((120,)), pltpu.SemaphoreType.DMA((120,))]
     anywhere = [pl.BlockSpec(memory_space=pltpu.HBM)]
     return pl.pallas_call(
         layer_kernel,
@@ -988,7 +1011,7 @@
             shaped((16, model), F32),
         ),
         in_specs=anywhere * (4 + len(vectors) + len(weights)),
-        out_specs=vmem(9),
+        out_specs=anywhere * 9,
         scratch_shapes=scratch,
         compiler_params=pltpu.CompilerParams(collective_id=0, has_side_effects=True, vmem_limit_bytes=62 * 2**20),
         name="layer",

time: 122 us -> 112 us (0.918); the launches traced: 122 us -> 110 us
  Pallas kernels: 121 us -> 109 us
    pallas_call x1, Pallas kernels: 112 us -> 100 us  [layer_call(): pl.pallas_call(layer_kernel, out_shape=(shaped((2, stretch, model), BF16)...]
where the time goes in v3:
time: 112 us; the launch traced here: 110 us
  Pallas kernels  109 us (97%)
    pallas_call x1, Pallas kernels, layer_call(): pl.pallas_call(layer_kernel, out_shape=(shaped((2, stretch, model), BF16)...  100 us
    pallas_call x1, Pallas kernels, finish(): pl.pallas_call(functools.partial(finish_kernel, parts), grid=(model // 12...  9.08 us

profile of v3, /device:TPU:9, one launch (start us, length us, event | category | flops | bytes accessed | tf_op | source)
XLA Modules:
  0.0 110.0 jit_solution(11214270321167337445)
XLA Ops:
  0.7 100.1 %layer.1 = (bf16[2,256,768]{2,1,0:T(8,128)(2,1)}, f32[2,256,768]{2,1,0:T(8,128)}, bf16[768,768]{1,0:T(8,128)(2,1)}, bf16[768,768]{1,0:T(8,128)(2,1)}, bf16[768,7...) custom-call(bf16[2,256,768]{2,1,0:T(8,128)(2,1)} %tokens.1, ...), custom_call_target="tpu_custom_call" | custom-call | tf_op jit(solution)/shard_map/layer/pallas_call | solution.py:1000
  100.7 9.1 %finish.1 = (f32[768,768]{1,0:T(8,128)}, f32[768,768]{1,0:T(8,128)}, f32[768,768]{1,0:T(8,128)}, f32[768,768]{1,0:T(8,128)}, bf16[2,256,768]{2,1,0:T(8,128)(2,1)...) custom-call(bf16[768,768]{1,0:T(8,128)(2,1)} %get-tuple-element.43.g, ...), custom_call_target="tpu_custom_call" | custom-call | tf_op jit(solution)/shard_map/finish/pallas_call | solution.py:932

commit v4 on v3

--- a/solution.py
+++ b/solution.py
@@ -20,20 +20,22 @@
     "p0": ("Sr10", "Sr11"),
     "p1": ("Sr20", "Sr21"),
     "p2": ("Sr30", "Sr31", "Er00", "Sr02"),
-    "dx": ("Ss0", "Er10", "Sr12", "Er01", "Er11", "Er20", "Sr22"),
-    "a1": ("Ed", "Si0", "Ef", "Es0", "Ss1", "Er21", "Er02", "Sr03"),
-    "a2": ("Er22", "Sr23", "Er30", "Sr32", "EH", "Si1", "Sh0", "Es1", "Ss2", "Ei0", "Er12", "Sr13", "Er03", "Sg03", "Er31", "Er23", "Sg23", "Er32", "Sr33"),
-    "a4": ("Sh1",),
-    "a5": ("Er13", "Sg13", "Ei1"),
-    "a6": ("Es2", "Ss3", "Eg03", "Sg00", "Sg02"),
-    "a9": ("Eg23", "Sg20", "Sg22"),
-    "a11": ("Er33", "Sg33"),
-    "f0": ("Eg00",),
-    "f1": ("Eg13", "Sg10", "Sg12", "Eh"),
-    "f2": ("Es3", "Eg20", "Eg02", "St00", "Sg01"),
-    "f4": ("So0", "Eg22", "St20", "Sg21", "Eg33", "Sg30", "Sg32", "Et00", "Eg12", "St10", "Sg11"),
-    "f6": ("Et20", "Eg10", "Eg01", "St01", "Et10"),
-    "end": ("Eg21", "St21", "Et01", "Eo0", "So1", "Et21", "Eg30", "Eg32", "St30", "Sg31", "Et30", "Eg11", "St11", "Eg31", "St31", "Et11", "Eo1", "Et31"),
+    "dx": ("Ss0", "Er10", "Sr12", "Er01"),
+    "a0": ("Er11",),
+    "a1": ("Er20", "Sr22"),
+    "a2": ("Ed", "Si0", "Es0", "Ss1", "Er02", "Sr03"),
+    "a3": ("Ef", "Er21"),
+    "a5": ("Er30", "Sr32", "Er22", "Sr23"),
+    "a6": ("Er03", "Sg03", "EH", "Si1", "Sh0", "Es1", "Ss2", "Er12", "Sr13", "Er31", "Er23", "Sg23", "Ei0"),
+    "a7": ("Er32", "Sr33"),
+    "a8": ("Eg03", "Sg00", "Sg02"),
+    "a11": ("Er13", "Sg13", "Sh1", "Ei1"),
+    "f0": ("Es2", "Ss3", "Eg02", "St00", "Sg01", "Eg23", "Sg20", "Sg22", "Eh0"),
+    "f2": ("Et00", "Eg00", "Er33", "Sg33"),
+    "f4": ("Eg13", "Sg10", "Sg12", "Eg22", "St20", "Sg21"),
+    "f6": ("Es3", "Et20", "Eh1"),
+    "f7": ("So0",),
+    "end": ("Eg33", "Sg30", "Sg32", "Eg01", "St01", "Ek", "Et01", "Eg20", "Eg10", "Em", "So1", "Eg12", "St10", "Sg11", "Eo0", "Et10", "Eg21", "St21", "Eg32", "St30", "Sg31", "Et21", "Eg30", "Et30", "Eo1", "Eg31", "St31", "Eg11", "St11", "Et31", "Et11"),
 }
 
 
@@ -299,7 +301,7 @@
     layer_out, input_grad, out_o, out_0, out_1, out_2, up_out, down_out, small_out,
     segments, slots, up_bias, bq, bv, bo, g1, s1, bdown, g2, s2, vecs, wq_t, wkv_t, wo_t, keys_t, values_t,
     xs, xs_t, cots, cot_part, cot_in, cot_sum, cot_far, dx_send, dx_in, wq_v, wk_v, wv_v, wo_v, wup_v, wdown_v, keys, values, queries, context, probs, picked, chosen, ctx_both, gb_both,
-    slopes, dq_low, dkv_low, grads, hidden_grads, hidden_in, fac_normed, fac_feed, grad_h1, small_in, small_z,
+    slopes, dq_low, dkv_low, grads, hidden_grads, hidden_in, hidden_far, hidden_share, hidden_got, fac_normed, fac_feed, grad_h1, small_in, small_z,
     all_queries, all_context, ctx_in, total, y1_keep, out_send, igrad_send, igrad_in,
     in_o, in_0, in_1, in_2, local_sem, send_sem, recv_sem,
 ):
@@ -359,8 +361,7 @@
     get_up = local(wup, wup_v, 6)
     get_down = local(wdown, wdown_v, 7)
 
-    near = [(1 - x, y), (x, 1 - y), (1 - x, 1 - y)]
-    greeted = [twin] + columns + [device(z, nx, ny, c) for nx, ny in near for c in range(2)]
+    greeted = [twin, at_x, at_y] + columns
     barrier = pltpu.get_barrier_semaphore()
     for target in greeted:
         pl.semaphore_signal(barrier, inc=1, device_id=target, device_id_type=MESH)
@@ -603,8 +604,6 @@
         else:
             small_out[...] = (small_z[0] + small_z[1]) + (small_z[2] + small_z[3])
 
-    source = x * 2 + y
-
     def factor_copies():
         return [remote(ref.at[core], ref.at[core], 22 + k, twin) for k, ref in enumerate((fac_normed, fac_feed))]
 
@@ -614,15 +613,20 @@
         for copy in factor_copies():
             copy.start()
 
-    def is_me(cy, cc):
-        return (core == x) & (cy == y) & (cc == core)
-
-    def hidden_copy(cy, cc):
-        part = hidden_grads.at[pl.ds((cy * 2 + cc) * units, units)]
-        return pltpu.make_async_remote_copy(
-            src_ref=part, dst_ref=hidden_in.at[source], send_sem=send_sem.at[24 + cy * 2 + cc], recv_sem=recv_sem.at[24 + source],
-            device_id=device(z, core, cy, cc), device_id_type=MESH,
-        )
+    two = 2 * units
+    summing = core == x
+
+    def part_at(which):
+        return pl.ds(pl.multiple_of(which * two, 16), two)
+
+    def across_copy(k):
+        return remote(hidden_grads.at[part_at(y if k else 1 - y)], hidden_in.at[k], 24 + k, at_x)
+
+    def along_copy():
+        return remote(hidden_grads.at[part_at(1 - y)], hidden_far, 26, at_y)
+
+    def share_copy():
+        return remote(hidden_share, hidden_got, 27, twin)
 
     def hidden_make():
         for copy in factor_copies():
@@ -636,38 +640,48 @@
         gp = (dot_nt(feed, wdown_v[at, :]) * slope).astype(BF16)
         hidden_grads[:, :model] = dot_tn(gp, normed).astype(BF16)
         hidden_grads[:, model:] = dot_tn(act.astype(BF16), feed).astype(BF16)
-        for cy in range(2):
-            for cc in range(2):
-                @pl.when(is_me(cy, cc))
-                def _(cy=cy, cc=cc):
-                    hidden_in[source] = hidden_grads[pl.ds((cy * 2 + cc) * units, units)]
-
-    def hidden_start(cc):
-        for cy in range(2):
-            @pl.when(jnp.logical_not(is_me(cy, cc)))
-            def _(cy=cy):
-                hidden_copy(cy, cc).start()
+
+    def hidden_start(k):
+        @pl.when(jnp.logical_not(summing))
+        def _():
+            across_copy(k).start()
+
+    def hidden_arrive(k):
+        @pl.when(jnp.logical_not(summing))
+        def _():
+            across_copy(k).wait_send()
+
+        @pl.when(summing)
+        def _():
+            across_copy(k).wait_recv()
+            if k == 0:
+                here = part_at(1 - y)
+                hidden_grads[here] = (hidden_grads[here].astype(F32) + hidden_in[0].astype(F32)).astype(BF16)
+                along_copy().start()
+
+    def hidden_sum():
+        @pl.when(summing)
+        def _():
+            along_copy().wait()
+            value = hidden_grads[part_at(y)].astype(F32) + hidden_in[1].astype(F32) + hidden_far[...].astype(F32)
+            low_part, high_part = value[:units], value[units:]
+            own = jnp.where(core == 0, low_part, high_part)
+            hidden_share[...] = jnp.where(core == 0, high_part, low_part).astype(BF16)
+            share_copy().start()
+            up_out[...] = own[:, :model]
+            down_out[...] = own[:, model:]
 
     def hidden_end():
-        for cy in range(2):
-            for cc in range(2):
-                @pl.when(jnp.logical_not(is_me(cy, cc)))
-                def _(cy=cy, cc=cc):
-                    hidden_copy(cy, cc).wait_send()
-        for cx in range(2):
-            for cy in range(2):
-                @pl.when(jnp.logical_not((cx == x) & (cy == y) & (core == x)))
-                def _(cx=cx, cy=cy):
-                    slot = hidden_in.at[cx * 2 + cy]
-                    pltpu.make_async_remote_copy(
-                        src_ref=slot, dst_ref=slot, send_sem=send_sem.at[24], recv_sem=recv_sem.at[24 + cx * 2 + cy],
-                        device_id=twin, device_id_type=MESH,
-                    ).wait_recv()
-        value = hidden_in[0].astype(F32)
-        for k in range(1, 4):
-            value = value + hidden_in[k].astype(F32)
-        up_out[...] = value[:, :model]
-        down_out[...] = value[:, model:]
+        @pl.when(summing)
+        def _():
+            share_copy().wait_send()
+
+        @pl.when(jnp.logical_not(summing))
+        def _():
+            share_copy().wait_recv()
+            value = hidden_got[...].astype(F32)
+            up_out[...] = value[:, :model]
+            down_out[...] = value[:, model:]
 
     def piece_of(index):
         return pl.ds(index * piece, piece)
@@ -729,9 +743,11 @@
             factors_on()
         elif kind == "H":
             hidden_make()
-        elif kind == "h" and start:
-            hidden_start(*rest)
         elif kind == "h":
+            (hidden_start if start else hidden_arrive)(*rest)
+        elif kind == "k":
+            hidden_sum()
+        elif kind == "m":
             hidden_end()
             result_copy(6).start()
             result_copy(7).start()
@@ -897,47 +913,84 @@
     return call
 
 
-def finish_kernel(parts, go, g0, g1, g2, layer_in, igrad_in, up_in, down_in, small, wq, wk, wv, wo, layer_out, igrad, up, down, up_bias, *vectors):
-    wo[...] = go[...].T.astype(F32)
-    for pair, ref in enumerate((g0, g1, g2)):
-        for core in range(2):
-            at = core * 384 + pair * 128
-            for place, out in enumerate((wq, wk, wv)):
-                begin = core * 384 + place * 128
-                out[:, at : at + 128] = ref[:, begin : begin + 128].astype(F32)
-    layer_out[...] = layer_in[...]
-    igrad[...] = igrad_in[...]
-    up[...] = up_in[...]
-    down[...] = down_in[...]
-
-    @pl.when(pl.program_id(0) == 0)
-    def _():
-        model = small.shape[1]
-        for part in range(parts):
-            up_bias[part * model : (part + 1) * model] = small[part]
-        for place, out in enumerate(vectors):
-            out[...] = small[parts + place]
+def finish_kernel(parts, go, g0, g1, g2, layer_in, igrad_in, up_in, down_in, small_in, wq, wk, wv, wo, layer_out, igrad, up, down, up_bias, *rest):
+    vectors, (go_v, pair_v, small, wide, wo_v, *through, in_sem, out_sem) = rest[:8], rest[8:]
+    model = go_v.shape[0]
+    width, tile = model // 2, 128
+    steps = model // tile
+    loads = [pltpu.make_async_copy(small_in, small, in_sem.at[0])]
+    for step in range(steps):
+        rows = pl.ds(step * tile, tile)
+        for pair, ref in enumerate((g0, g1, g2)):
+            loads.append(pltpu.make_async_copy(ref.at[rows], pair_v.at[pair, rows], in_sem.at[1 + step * 3 + pair]))
+    loads.append(pltpu.make_async_copy(go, go_v, in_sem.at[1 + 3 * steps]))
+    passed = tuple(zip((igrad_in, layer_in, up_in, down_in), through, (igrad, layer_out, up, down)))
+    for index, (src, held, _) in enumerate(passed):
+        loads.append(pltpu.make_async_copy(src, held, in_sem.at[2 + 3 * steps + index]))
+    for copy in loads:
+        copy.start()
+    stores = []
+
+    def store(src, dst):
+        copy = pltpu.make_async_copy(src, dst, out_sem.at[len(stores)])
+        copy.start()
+        stores.append(copy)
+
+    loads[0].wait()
+    for part in range(parts):
+        up_bias[part * model : (part + 1) * model] = small[part]
+    for place, out in enumerate(vectors):
+        out[...] = small[parts + place]
+    for step in range(steps):
+        rows = pl.ds(step * tile, tile)
+        for pair in range(3):
+            loads[1 + step * 3 + pair].wait()
+            for core in range(2):
+                to = core * width + pair * 128
+                for place in range(3):
+                    begin = core * width + place * 128
+                    wide[place, rows, to : to + 128] = pair_v[pair, rows, begin : begin + 128].astype(F32)
+        for place, out in enumerate((wq, wk, wv)):
+            store(wide.at[place, rows], out.at[rows])
+    for index, (_, held, dst) in enumerate(passed):
+        loads[2 + 3 * steps + index].wait()
+        store(held, dst)
+    loads[1 + 3 * steps].wait()
+    for step in range(steps):
+        rows = pl.ds(step * tile, tile)
+        wo_v[rows, :] = go_v[:, step * tile : (step + 1) * tile].T.astype(F32)
+        store(wo_v.at[rows], wo.at[rows])
+    for copy in stores:
+        copy.wait()
 
 
 def finish(layer_output, input_grad, go, g0, g1, g2, up_part, down_part, small, hidden):
     model = go.shape[0]
-    stretch, units, parts = layer_output.shape[1], up_part.shape[0], hidden // model
+    parts, steps = hidden // model, model // 128
     shaped = jax.ShapeDtypeStruct
-    rows = pl.BlockSpec((128, model), lambda i: (i, 0))
-    columns = pl.BlockSpec((model, 128), lambda i: (0, i))
-    tokens = pl.BlockSpec((2, stretch, 128), lambda i: (0, 0, i))
-    unit = pl.BlockSpec((units, 128), lambda i: (0, i))
-    line = pl.BlockSpec((model,), lambda i: (0,))
     square, vector = shaped((model, model), F32), shaped((model,), F32)
+    far = pl.BlockSpec(memory_space=pltpu.HBM)
     found = pl.pallas_call(
         functools.partial(finish_kernel, parts),
-        grid=(model // 128,),
         out_shape=(square,) * 4
         + (shaped(layer_output.shape, BF16), shaped(input_grad.shape, F32), shaped(up_part.shape, F32), shaped(down_part.shape, F32))
         + (shaped((hidden,), F32),)
         + (vector,) * 8,
-        in_specs=[columns, rows, rows, rows, tokens, tokens, unit, unit, pl.BlockSpec(small.shape, lambda i: (0, 0))],
-        out_specs=[rows] * 4 + [tokens, tokens, unit, unit, pl.BlockSpec((hidden,), lambda i: (0,))] + [line] * 8,
+        in_specs=[far] * 9,
+        out_specs=[far] * 8 + vmem(9),
+        scratch_shapes=[
+            pltpu.VMEM((model, model), BF16),
+            pltpu.VMEM((3, model, model), BF16),
+            pltpu.VMEM(small.shape, F32),
+            pltpu.VMEM((3, model, model), F32),
+            pltpu.VMEM((model, model), F32),
+            pltpu.VMEM(input_grad.shape, F32),
+            pltpu.VMEM(layer_output.shape, BF16),
+            pltpu.VMEM(up_part.shape, F32),
+            pltpu.VMEM(down_part.shape, F32),
+            pltpu.SemaphoreType.DMA((6 + 3 * steps,)),
+            pltpu.SemaphoreType.DMA((4 + 4 * steps,)),
+        ],
         compiler_params=pltpu.CompilerParams(vmem_limit_bytes=VMEM_LIMIT),
         name="finish",
     )(go, g0, g1, g2, layer_output, input_grad, up_part, down_part, small)
@@ -989,7 +1042,7 @@
         low(model, hidden), low(hidden, model), low(full, width), low(full, width), low(count, width), low(count, width),
         low(HEADS // 2, count, full), low(count, model), low(count, full), low(2, masks, width), low(2, masks, model),
         wide(hidden // model, masks, model), low(count, width), low(full, model), low(4, model, width),
-        low(4 * units, 2 * model), low(4, units, 2 * model), low(2, 4, masks, model), low(2, 4, masks, model),
+        low(4 * units, 2 * model), low(2, 2 * units, 2 * model), low(2 * units, 2 * model), low(units, 2 * model), low(units, 2 * model), low(2, 4, masks, model), low(2, 4, masks, model),
         wide(masks, model), wide(7, 16, model), wide(4, 16, model),
         low(full, width), low(full, width), low(half, width), wide(stretch, model), low(stretch, model), low(stretch, model),
         low(stretch, model), low(stretch, model),

time: 112 us -> 108 us (0.964); the launches traced: 110 us -> 108 us
  Pallas kernels: 109 us -> 107 us
    pallas_call x1, Pallas kernels: 100 us -> 98.6 us  [layer_call(): pl.pallas_call(layer_kernel, out_shape=(shaped((2, stretch, model), BF16)...]
where the time goes in v4:
time: 108 us
  Pallas kernels  107 us (99%)
    pallas_call x1, Pallas kernels, layer_call(): pl.pallas_call(layer_kernel, out_shape=(shaped((2, stretch, model), BF16)...  98.6 us
    pallas_call x1, Pallas kernels, finish(): pl.pallas_call(functools.partial(finish_kernel, parts), out_shape=(square...  8.56 us

profile of v4, /device:TPU:9, one launch (start us, length us, event | category | flops | bytes accessed | tf_op | source)
XLA Modules:
  0.0 108.0 jit_solution(18059535363514139960)
XLA Ops:
  0.7 98.6 %layer.1 = (bf16[2,256,768]{2,1,0:T(8,128)(2,1)}, f32[2,256,768]{2,1,0:T(8,128)}, bf16[768,768]{1,0:T(8,128)(2,1)}, bf16[768,768]{1,0:T(8,128)(2,1)}, bf16[768,7...) custom-call(bf16[2,256,768]{2,1,0:T(8,128)(2,1)} %tokens.1, ...), custom_call_target="tpu_custom_call" | custom-call | tf_op jit(solution)/shard_map/layer/pallas_call | solution.py:1053
  99.3 8.6 %finish.1 = (f32[768,768]{1,0:T(8,128)}, f32[768,768]{1,0:T(8,128)}, f32[768,768]{1,0:T(8,128)}, f32[768,768]{1,0:T(8,128)}, bf16[2,256,768]{2,1,0:T(8,128)(2,1)...) custom-call(bf16[768,768]{1,0:T(8,128)(2,1)} %get-tuple-element.43.g, ...), custom_call_target="tpu_custom_call" | custom-call | tf_op jit(solution)/shard_map/finish/pallas_call | solution.py:973

commit v5 on v4

--- a/solution.py
+++ b/solution.py
@@ -16,26 +16,28 @@
 VMEM_LIMIT = 56 * 2**20
 ORDERS = ("xyz", "yxz", "xyz", "xyz")
 PLAN = {
-    "G0": ("Sr00", "Sr01"),
     "p0": ("Sr10", "Sr11"),
     "p1": ("Sr20", "Sr21"),
-    "p2": ("Sr30", "Sr31", "Er00", "Sr02"),
-    "dx": ("Ss0", "Er10", "Sr12", "Er01"),
-    "a0": ("Er11",),
-    "a1": ("Er20", "Sr22"),
-    "a2": ("Ed", "Si0", "Es0", "Ss1", "Er02", "Sr03"),
-    "a3": ("Ef", "Er21"),
-    "a5": ("Er30", "Sr32", "Er22", "Sr23"),
-    "a6": ("Er03", "Sg03", "EH", "Si1", "Sh0", "Es1", "Ss2", "Er12", "Sr13", "Er31", "Er23", "Sg23", "Ei0"),
-    "a7": ("Er32", "Sr33"),
-    "a8": ("Eg03", "Sg00", "Sg02"),
-    "a11": ("Er13", "Sg13", "Sh1", "Ei1"),
-    "f0": ("Es2", "Ss3", "Eg02", "St00", "Sg01", "Eg23", "Sg20", "Sg22", "Eh0"),
-    "f2": ("Et00", "Eg00", "Er33", "Sg33"),
-    "f4": ("Eg13", "Sg10", "Sg12", "Eg22", "St20", "Sg21"),
-    "f6": ("Es3", "Et20", "Eh1"),
-    "f7": ("So0",),
-    "end": ("Eg33", "Sg30", "Sg32", "Eg01", "St01", "Ek", "Et01", "Eg20", "Eg10", "Em", "So1", "Eg12", "St10", "Sg11", "Eo0", "Et10", "Eg21", "St21", "Eg32", "St30", "Sg31", "Et21", "Eg30", "Et30", "Eo1", "Eg31", "St31", "Eg11", "St11", "Et31", "Et11"),
+    "G0": ("Sr02",),
+    "p2": ("Sr30", "Sr31", "Er10", "Sr12"),
+    "dx": ("Ss0", "Er11", "Er20", "Sr22"),
+    "a0": ("Er21", "Er02", "Sr03"),
+    "a1": ("Ed", "Si0", "Es0", "Ss1", "Ef", "Er30", "Sr32"),
+    "a2": ("Er22", "Sr23"),
+    "a3": ("Er31", "Er03", "Sg03", "EH", "Sh0", "Si1", "Es1", "Ss2", "Er12", "Sr13", "Er23", "Sg23", "Ei0"),
+    "a4": ("Er32", "Sr33", "Eg03", "Sg00", "Sg02"),
+    "a6": ("Er13", "Sg13"),
+    "a7": ("Ei1",),
+    "a8": ("Sh1", "Es2", "Ss3", "Eh0", "Eg23", "Sg20", "Sg22"),
+    "a9": ("Eg02", "St00", "Sg01"),
+    "a10": ("Er33", "Sg33", "Eg00", "Et00"),
+    "f0": ("Eg13", "Sg10", "Sg12"),
+    "f2": ("Es3", "Eh1", "Ek"),
+    "f3": ("So0", "Eg22", "St20", "Sg21"),
+    "f4": ("Em", "Eg33", "Sg30", "Sg32", "Et20", "Eg20"),
+    "f5": ("Eg10",),
+    "f6": ("Eg01", "St01"),
+    "end": ("Et01", "So1", "Eo0", "Eg12", "St10", "Sg11", "Et10", "Eg32", "St30", "Sg31", "Eg21", "St21", "Et30", "Et21", "Eg30", "Eo1", "Eg31", "St31", "Eg11", "St11", "Et31", "Et11"),
 }
 
 
@@ -300,7 +302,7 @@
     layer_hbm, igrad_hbm, hbm_o, hbm_0, hbm_1, hbm_2, up_hbm, down_hbm, small_hbm,
     layer_out, input_grad, out_o, out_0, out_1, out_2, up_out, down_out, small_out,
     segments, slots, up_bias, bq, bv, bo, g1, s1, bdown, g2, s2, vecs, wq_t, wkv_t, wo_t, keys_t, values_t,
-    xs, xs_t, cots, cot_part, cot_in, cot_sum, cot_far, dx_send, dx_in, wq_v, wk_v, wv_v, wo_v, wup_v, wdown_v, keys, values, queries, context, probs, picked, chosen, ctx_both, gb_both,
+    xs, xs_t, cots, cot_part, cot_in, cot_sum, cot_far, dx_send, dx_in, wq_v, wk_v, wv_v, wo_v, wup_v, wdown_v, keys, values, queries, context, probs, picked, chosen, ctx_both, ctx_far, gb_both, gb_far,
     slopes, dq_low, dkv_low, grads, hidden_grads, hidden_in, hidden_far, hidden_share, hidden_got, fac_normed, fac_feed, grad_h1, small_in, small_z,
     all_queries, all_context, ctx_in, total, y1_keep, out_send, igrad_send, igrad_in,
     in_o, in_0, in_1, in_2, local_sem, send_sem, recv_sem,
@@ -387,9 +389,12 @@
         block_values = (dot(block, wv_v[...]) + half_vector(5)).astype(BF16)
         keys[here, :] = block_keys
         values[here, :] = block_values
-        xs_t[:, here] = block.T
         keys_t[:, here] = block_keys.T
-        values_t[:, here] = block_values.T
+
+    def turn_tokens(start):
+        here = pl.ds(start, stretch)
+        xs_t[:, here] = xs[here, :].T
+        values_t[:, here] = values[here, :].T
 
     blocks = [2 * y + core, 2 * (1 - y) + core, 2 * y + 1 - core, 2 * (1 - y) + 1 - core]
     lane = lax.broadcasted_iota(jnp.int32, (1, stretch), 1)
@@ -421,6 +426,8 @@
     key_values(0)
     tok_c.wait_recv()
     key_values(half)
+    turn_tokens(0)
+    turn_tokens(half)
     get_wq.wait()
     for pair in range(width // 128):
         lanes = slice(pair * 128, pair * 128 + 128)
@@ -464,10 +471,10 @@
         context[:, lanes] = jnp.where(first, outs[0], outs[1]).astype(BF16)
     ctx_both[core] = context[my_slots, :]
     ctx_c = push(context.at[twin_slots], ctx_both.at[core], 7, twin)
-
-    for start in range(0, full, stretch):
-        value = (dot(xs[start : start + stretch, :], wq_v[...]) + half_vector(4)).astype(BF16)
-        all_queries[start : start + stretch, :] = (value.astype(F32) * 0.125).astype(BF16)
+    ctx_x = push(context, ctx_far, 34, at_x)
+
+    turn_tokens(stretch)
+    turn_tokens(half + stretch)
     get_wo.wait()
     wo_t[...] = wo_v[mine, :].T
     ctx_c.wait_recv()
@@ -509,9 +516,14 @@
     gb = gh1.astype(BF16)
     gb_both[core] = gb
     gb_c = push(gb_both.at[core], gb_both.at[core], 15, twin)
+    for start in range(0, full, stretch):
+        value = (dot(xs[start : start + stretch, :], wq_v[...]) + half_vector(4)).astype(BF16)
+        all_queries[start : start + stretch, :] = (value.astype(F32) * 0.125).astype(BF16)
     for place, value in enumerate((gy1 * n1, gy1, grad * n2, grad, gb.astype(F32), gf.astype(F32))):
         small_in[0, parts + place : parts + place + 1, :] = jnp.sum(value, axis=0, keepdims=True)
     gb_c.wait_recv()
+    far_half = pl.ds(pl.multiple_of((1 - x) * width, 128), width)
+    gb_x = push(gb_both.at[:, :, far_half], gb_far, 35, at_x)
 
     spots = {"x": x, "y": y}
     neighbours = {"x": at_x, "y": at_y}
@@ -576,7 +588,9 @@
             grads[job, here] = (grads[job, here].astype(F32) + arrive[:quarter].astype(F32)).astype(BF16)
         elif stage == 2:
             here = at(mine_at, quarter)
-            value = grads[job, here].astype(F32) + arrive[quarter : 2 * quarter].astype(F32)
+            value = grads[job, here].astype(F32)
+            if job > 0:
+                value = value + arrive[quarter : 2 * quarter].astype(F32)
             grads[job, here] = (value + arrive[2 * quarter : 3 * quarter].astype(F32)).astype(BF16)
         elif stage == 3:
             value = grads[job, at(own, chunk)].astype(F32)
@@ -758,8 +772,6 @@
 
     gb = gb_both[...].reshape(count, model)
     gctx = dot(gb, wo_t[...]).astype(BF16)
-    grads[0] = dot_tn(gb, context[...]).astype(BF16)
-    act_on("G0")
     for pair in range(pairs):
         lanes = slice(pair * 128, pair * 128 + 128)
         pair_keys, pair_values, pair_queries = keys[:, lanes], values_t[lanes, :], queries[:, lanes]
@@ -788,6 +800,13 @@
         grads[1 + pair, :, :128] = dot_tn(picked[...], dq).astype(BF16)
         grads[1 + pair, :, 128:] = dot(xs_t[...], dkv_low[:, both]).astype(BF16)
         act_on("p" + str(pair))
+        if pair == 1:
+            ctx_x.wait_recv()
+            gb_x.wait_recv()
+            near_half = gb_both[:, :, pl.ds(pl.multiple_of(x * width, 128), width)].reshape(count, width)
+            value = dot_tn(near_half, context[...]) + dot_tn(gb_far[...].reshape(count, width), ctx_far[...])
+            grads[0, at(x * width, width)] = value.astype(BF16)
+            act_on("G0")
         there = pl.ds(pl.multiple_of(core * width + pair * 128, 128), 128)
         small_in[0, parts + 6 : parts + 7, there] = jnp.sum(dq.astype(F32), axis=0, keepdims=True)
         small_in[0, parts + 7 : parts + 8, there] = jnp.sum(dv.astype(F32), axis=0, keepdims=True)
@@ -1040,7 +1059,7 @@
         low(full, model), low(model, full), low(2, stretch, model), low(2, 2, masks, model), low(2, masks, model), low(2, masks, model),
         low(masks, model), low(half, model), low(half, model), low(model, width), low(model, width), low(model, width), low(model, model),
         low(model, hidden), low(hidden, model), low(full, width), low(full, width), low(count, width), low(count, width),
-        low(HEADS // 2, count, full), low(count, model), low(count, full), low(2, masks, width), low(2, masks, model),
+        low(HEADS // 2, count, full), low(count, model), low(count, full), low(2, masks, width), low(count, width), low(2, masks, model), low(2, masks, width),
         wide(hidden // model, masks, model), low(count, width), low(full, model), low(4, model, width),
         low(4 * units, 2 * model), low(2, 2 * units, 2 * model), low(2 * units, 2 * model), low(units, 2 * model), low(units, 2 * model), low(2, 4, masks, model), low(2, 4, masks, model),
         wide(masks, model), wide(7, 16, model), wide(4, 16, model),

time: 108 us -> 108 us (level); the launches traced: 108 us -> 106 us
    pallas_call x1, Pallas kernels: 98.6 us -> 97.1 us  [layer_call(): pl.pallas_call(layer_kernel, out_shape=(shaped((2, stretch, model), BF16)...]
where the time goes in v5:
time: 108 us; the launch traced here: 106 us
  Pallas kernels  106 us (98%)
    pallas_call x1, Pallas kernels, layer_call(): pl.pallas_call(layer_kernel, out_shape=(shaped((2, stretch, model), BF16)...  97.1 us
    pallas_call x1, Pallas kernels, finish(): pl.pallas_call(functools.partial(finish_kernel, parts), out_shape=(square...  8.56 us

profile of v5, /device:TPU:9, one launch (start us, length us, event | category | flops | bytes accessed | tf_op | source)
XLA Modules:
  0.0 106.5 jit_solution(4635353209358851972)
XLA Ops:
  0.7 97.1 %layer.1 = (bf16[2,256,768]{2,1,0:T(8,128)(2,1)}, f32[2,256,768]{2,1,0:T(8,128)}, bf16[768,768]{1,0:T(8,128)(2,1)}, bf16[768,768]{1,0:T(8,128)(2,1)}, bf16[768,7...) custom-call(bf16[2,256,768]{2,1,0:T(8,128)(2,1)} %tokens.1, ...), custom_call_target="tpu_custom_call" | custom-call | tf_op jit(solution)/shard_map/layer/pallas_call | solution.py:1072
  97.8 8.6 %finish.1 = (f32[768,768]{1,0:T(8,128)}, f32[768,768]{1,0:T(8,128)}, f32[768,768]{1,0:T(8,128)}, f32[768,768]{1,0:T(8,128)}, bf16[2,256,768]{2,1,0:T(8,128)(2,1)...) custom-call(bf16[768,768]{1,0:T(8,128)(2,1)} %get-tuple-element.43.g, ...), custom_call_target="tpu_custom_call" | custom-call | tf_op jit(solution)/shard_map/finish/pallas_call | solution.py:992
